TPU v7x, 32 devices: a whole 2x2x4 slice. The times are simulated.
32 devices in a mesh: wide: 16 (over z, y, core), grp: 2 (over x).
Axes of the slice: x: 2, y: 2, z: 4, core: 2. Of those that a mesh axis runs over, the one named last changes fastest.
Arguments:
- tokens: bfloat16 [65536, 128], P(('grp', 'wide')), parts along dimension 0, may hold values from -6 to 6
- cotangent: bfloat16 [65536, 128], P(('grp', 'wide')), parts along dimension 0, may hold values from -6 to 6
- order_send: int32 [65536], P(('grp', 'wide')), parts along dimension 0, may hold values from 0 to 2047, as said below
- order_recv: int32 [65536], P(('grp', 'wide')), parts along dimension 0, may hold values from 0 to 2047, as said below
- gain_a: float32 [128], replicated, may hold values from 0.1 to 1.9
- qkv_a: bfloat16 [128, 384], replicated, may hold values from -0.35355339 to 0.35355339
- proj_a: bfloat16 [128, 128], replicated, may hold values from -0.5 to 0.5
- gain_b: float32 [128], replicated, may hold values from 0.1 to 1.9
- qkv_b: bfloat16 [128, 384], replicated, may hold values from -0.35355339 to 0.35355339
- proj_b: bfloat16 [128, 128], replicated, may hold values from -0.5 to 0.5
Outputs:
- d_tokens: bfloat16 [65536, 128], P(('grp', 'wide')), parts along dimension 0
- d_gain_a: float32 [256], P('grp'), parts along dimension 0
- d_qkv_a: float32 [256, 384], P('grp'), parts along dimension 0
- d_proj_a: float32 [256, 128], P('grp'), parts along dimension 0
- d_gain_b: float32 [256], P('grp'), parts along dimension 0
- d_qkv_b: float32 [256, 384], P('grp'), parts along dimension 0
- d_proj_b: float32 [256, 128], P('grp'), parts along dimension 0
There are 2 independent parts, one for each index of `grp`. A program takes and returns all parts, laid end to end along the dimension named above; an argument that names none is the same for every part. Nothing has to cross between parts.
Inputs may be any that keep to these rules, and one draw needn't show every extreme that they name: Within every block of 2048 entries, order_send is a permutation of 0 to 2047. Within every block of 2048 entries, order_recv is a permutation of 0 to 2047.
All inputs are finite; a program needn't handle non-finite values.
Results may differ from a plain program's by a relative error of at most 0.03.
Values may be sent and summed in bfloat16 or wider, within the bound.
No kernel may reach another device: no remote copies, remote signals or barrier semaphores. Data moves between devices by JAX's collectives and lax.ppermute only.
A program may use at most 192 MiB of HBM per device.

v0:
```python
import jax
import jax.numpy as jnp
from jax import lax
from jax.sharding import PartitionSpec as P

D = 128
HEADS = 8
BALL = 256
HEAD_DIM = 16


def norm_rows(values, gain):
    mean_sq = jnp.mean(values * values, axis=-1, keepdims=True)
    return values * lax.rsqrt(mean_sq + 1e-06) * gain


def ball_core(qkv):
    rows = qkv.shape[0]
    balls = qkv.reshape(rows // BALL, BALL, 3, HEADS, HEAD_DIM)
    query = balls[:, :, 0]
    keys = balls[:, :, 1]
    values = balls[:, :, 2]
    scores = jnp.einsum(
        "bqhd,bkhd->bhqk", query, keys, preferred_element_type=jnp.float32
    ) * HEAD_DIM ** (-0.5)
    weights = jax.nn.softmax(scores, axis=-1).astype(jnp.bfloat16)
    attended = jnp.einsum("bhqk,bkhd->bqhd", weights, values, preferred_element_type=jnp.float32)
    return attended.reshape(rows, D)


def block_forward(rows_in, gain, w_qkv, w_proj):
    values = rows_in.astype(jnp.float32)
    normed = norm_rows(values, gain).astype(jnp.bfloat16)
    qkv = jnp.dot(normed, w_qkv, preferred_element_type=jnp.float32).astype(jnp.bfloat16)
    attended = ball_core(qkv).astype(jnp.bfloat16)
    return (values + jnp.dot(attended, w_proj, preferred_element_type=jnp.float32)).astype(
        jnp.bfloat16
    )


def block_backward(rows_in, gain, w_qkv, w_proj, d_out):
    values = rows_in.astype(jnp.float32)
    normed_f, norm_back = jax.vjp(norm_rows, values, gain)
    normed = normed_f.astype(jnp.bfloat16)
    qkv = jnp.dot(normed, w_qkv, preferred_element_type=jnp.float32).astype(jnp.bfloat16)
    attended_f, core_back = jax.vjp(ball_core, qkv)
    attended = attended_f.astype(jnp.bfloat16)
    d_proj = jnp.dot(attended.T, d_out, preferred_element_type=jnp.float32)
    d_att = jnp.dot(d_out, w_proj.T, preferred_element_type=jnp.float32).astype(jnp.bfloat16)
    d_rows_qkv = core_back(d_att.astype(jnp.float32))[0]
    d_qkv = jnp.dot(normed.T, d_rows_qkv, preferred_element_type=jnp.float32)
    d_normed = jnp.dot(d_rows_qkv, w_qkv.T, preferred_element_type=jnp.float32)
    d_values, d_gain = norm_back(d_normed)
    d_in = (d_out.astype(jnp.float32) + d_values).astype(jnp.bfloat16)
    return (d_in, d_gain, d_qkv, d_proj)


def body(tokens, cotangent, order_send, order_recv, gain_a, qkv_a, proj_a, gain_b, qkv_b, proj_b):
    rows = tokens.shape[0]
    width = tokens.shape[1]
    peers = lax.axis_size("wide")
    first = block_forward(tokens, gain_a, qkv_a, proj_a)
    outgoing = jnp.take(first, order_send, axis=0).reshape(peers, rows // peers, width)
    incoming = lax.all_to_all(outgoing, "wide", split_axis=0, concat_axis=0, tiled=True).reshape(
        rows, width
    )
    rotated = jnp.take(incoming, order_recv, axis=0)
    d_rotated, d_gain_b, d_qkv_b, d_proj_b = block_backward(
        rotated, gain_b, qkv_b, proj_b, cotangent
    )
    d_incoming = jnp.zeros((rows, width), jnp.bfloat16).at[order_recv].set(d_rotated)
    returned = lax.all_to_all(
        d_incoming.reshape(peers, rows // peers, width),
        "wide",
        split_axis=0,
        concat_axis=0,
        tiled=True,
    ).reshape(rows, width)
    d_first = jnp.zeros((rows, width), jnp.bfloat16).at[order_send].set(returned)
    d_tokens, d_gain_a, d_qkv_a, d_proj_a = block_backward(tokens, gain_a, qkv_a, proj_a, d_first)
    d_gain_a, d_qkv_a, d_proj_a, d_gain_b, d_qkv_b, d_proj_b = lax.psum(
        (d_gain_a, d_qkv_a, d_proj_a, d_gain_b, d_qkv_b, d_proj_b), "wide"
    )
    return (d_tokens, d_gain_a, d_qkv_a, d_proj_a, d_gain_b, d_qkv_b, d_proj_b)


def solution(mesh):
    return jax.shard_map(
        body,
        mesh=mesh,
        in_specs=(
            P(("grp", "wide"), None),
            P(("grp", "wide"), None),
            P(("grp", "wide")),
            P(("grp", "wide")),
            P(),
            P(),
            P(),
            P(),
            P(),
            P(),
        ),
        out_specs=(
            P(("grp", "wide"), None),
            P("grp"),
            P("grp", None),
            P("grp", None),
            P("grp"),
            P("grp", None),
            P("grp", None),
        ),
        check_vma=False,
    )
```

profile of v0, /device:TPU:0, one launch (start us, length us, event | category | flops | bytes accessed | tf_op | source)
XLA Modules:
  0.0 330.9 jit_solution(5913875355227245358)
XLA Ops:
  8.6 1.4 fusion.47
  11.2 1.7 convolution_convert_fusion.3
  14.4 9.0 %fusion.79 = (f32[8,8,256]{2,1,0:T(8,128)S(1)}, f32[8,8,256,256]{2,3,1,0:T(8,128)}) fusion(bf16[8,256,1,8,16]{1,0,4,3,2:T(8,128)(2,1)S(1)} %get-tuple-element.24, bf16[8,256,1,8,16]{1,0,4,3,2:T(8,128)(2,1)S(1)} %get-tuple-element.25), kind=kOutput, calls=%fused_computation.125 | convolution fusion | flops 146800896 | bytes 17891328 | tf_op jit(solution)/shard_map/sub | solution.py:26
  23.3 6.8 %divide_convert_fusion.1 = bf16[8,8,256,256]{2,3,1,0:T(8,128)(2,1)S(1)} fusion(f32[8,8,256,256]{2,3,1,0:T(8,128)} %get-tuple-element.31, f32[8,8,256]{2,1,0:T(8,128)S(1)} %get-tuple-element.30), kind=kLoop, calls=%fused_computation.22 | loop fusion | flops 8388608 | bytes 25231360 | tf_op jit(solution)/shard_map/convert_element_type | solution.py:26
  30.3 3.2 copy-done.1
  33.4 1.2 fusion.33
  35.4 6.2 %gather_fusion = bf16[2048,128]{1,0:T(8,128)(2,1)S(1)} fusion(bf16[2048,128]{1,0:T(8,128)(2,1)S(1)} %fusion.24, s32[2048]{0:T(1024)S(1)} %get-tuple-element.28), kind=kCustom, calls=%fused_computation.clone | custom fusion | bytes 1056768 | tf_op jit(solution)/shard_map/jit(_take)/gather | solution.py:63
  41.6 1.1 broadcast_select_fusion.1
  42.7 7.6 %all-to-all-start = ((bf16[16,128,128]{2,1,0:T(8,128)(2,1)}), bf16[16,128,128]{2,1,0:T(8,128)(2,1)S(1)}, u32[]{:S(2)}, u32[]{:S(2)}) async-start(bf16[16,128,128]{2,1,0:T(8,128)(2,1)} %bitcast.173), calls=%async_computation | async-start | bytes 1048576 | tf_op jit(solution)/shard_map/all_to_all | solution.py:64
  50.9 0.9 copy.73
  51.8 12.9 %all-to-all-done = bf16[16,128,128]{2,1,0:T(8,128)(2,1)S(1)} async-done(((bf16[16,128,128]{2,1,0:T(8,128)(2,1)}), bf16[16,128,128]{2,1,0:T(8,128)(2,1)S(1)}, u32[]{:S(2)}, u32[]{:S(2)}) %all-to-all-start) | async-done | bytes 524320 | tf_op jit(solution)/shard_map/all_to_all | solution.py:64
  64.8 6.2 %gather_fusion.1 = bf16[2048,128]{1,0:T(8,128)(2,1)S(1)} fusion(bf16[2048,128]{1,0:T(8,128)(2,1)S(1)} %bitcast.160, s32[2048]{0:T(1024)S(1)} %get-tuple-element.26), kind=kCustom, calls=%fused_computation.1.clone | custom fusion | bytes 1056768 | tf_op jit(solution)/shard_map/jit(_take)/gather | solution.py:67
  71.6 1.9 convolution_convert_fusion.2
  73.6 1.7 copy.40
  75.8 0.9 fusion.77
  76.7 9.0 %fusion.80 = (f32[8,8,256]{2,1,0:T(8,128)S(1)}, f32[8,8,256,256]{2,3,1,0:T(8,128)}) fusion(bf16[8,256,1,8,16]{1,0,4,3,2:T(8,128)(2,1)S(1)} %get-tuple-element.22, bf16[8,256,1,8,16]{1,0,4,3,2:T(8,128)(2,1)S(1)} %get-tuple-element.21), kind=kOutput, calls=%fused_computation.126 | convolution fusion | flops 146800896 | bytes 17891328 | tf_op jit(solution)/shard_map/jvp()/sub | solution.py:26
  85.7 10.9 %divide_convert_fusion = (bf16[8,8,256,256]{2,3,1,0:T(8,128)(2,1)S(1)}, f32[8,8,256]{2,1,0:T(8,128)}, bf16[8,8,256,256]{2,3,1,0:T(8,128)(2,1)}) fusion(f32[8,8,256,256]{2,3,1,0:T(8,128)} %get-tuple-element.33, f32[8,8,256]{2,1,0:T(8,128)S(1)} %get-tuple-element.32, f32[8,8,256]{2,1,0:T(8,128)S(1)} %multiply_divide_fusion.1, ...), kind=kOutput, calls=%fused_computation.20 | convolution fusion | flops 163561472 | bytes 34799616 | tf_op jit(solution)/shard_map/transpose(jvp(bhqk,bkhd->bqhd))/dot_general | solution.py:27
  96.7 0.9 neg.12
  97.6 12.2 %fusion.30 = bf16[8,256,1,8,16]{1,4,3,0,2:T(8,128)(2,1)S(1)} fusion(bf16[8,256,1,8,16]{1,0,4,3,2:T(8,128)(2,1)} %copy-done.17, f32[8,8,256,256]{2,3,1,0:T(8,128)} %get-tuple-element.33, bf16[8,8,256,256]{2,3,1,0:T(8,128)(2,1)} %get-tuple-element.34, f32[8,8,256]{2,1,0:T(8,128)S(1)} %neg.12, f32[8,8,256]{2,1,0:T(8,128)S(1)} %get-tuple-element.32), kind=kOutput, calls=%fused_computation.65 | convolution fusion | flops 155451392 | bytes 26345472 | tf_op jit(solution)/shard_map/transpose(jvp(bqhd,bkhd->bhqk))/dot_general | solution.py:23
  109.8 10.2 %fusion.29 = bf16[8,256,1,8,16]{1,4,3,0,2:T(8,128)(2,1)S(1)} fusion(bf16[8,256,1,8,16]{1,0,4,3,2:T(8,128)(2,1)S(1)} %copy-done.16, f32[8,8,256,256]{2,3,1,0:T(8,128)} %get-tuple-element.33, bf16[8,8,256,256]{2,3,1,0:T(8,128)(2,1)} %get-tuple-element.34, f32[8,8,256]{2,1,0:T(8,128)S(1)} %neg.12, f32[8,8,256]{2,1,0:T(8,128)S(1)} %get-tuple-element.32), kind=kOutput, calls=%fused_computation.64 | convolution fusion | flops 155451392 | bytes 26345472 | tf_op jit(solution)/shard_map/transpose(jvp(bqhd,bkhd->bhqk))/dot_general | solution.py:23
  120.0 2.3 fusion.34
  122.4 0.9 copy.49
  123.8 1.2 copy-done.11
  125.0 1.5 fusion.40
  126.5 8.5 %scatter_custom_fusion = bf16[2048,128]{1,0:T(8,128)(2,1)} fusion(s32[2048]{0:T(1024)S(1)} %get-tuple-element.27, bf16[2048,128]{1,0:T(8,128)(2,1)} %param.13, f32[2048,128]{1,0:T(8,128)S(1)} %get-tuple-element.35, f32[2048]{0:T(1024)S(1)} %multiply_multiply_fusion.1, f32[128]{0:T(128)S(1)} %copy-done.27, f32[2048]{0:T(1024)S(1)} %fusion.70, ...), kind=kCustom, calls=%fused_computation.84 | custom fusion | flops 2621440 | bytes 2640386 | tf_op jit(solution)/shard_map/scatter | solution.py:71
  134.9 4.2 %all-to-all-start.1 = ((bf16[16,128,128]{2,1,0:T(8,128)(2,1)}), bf16[16,128,128]{2,1,0:T(8,128)(2,1)}, u32[]{:S(2)}, u32[]{:S(2)}) async-start(bf16[16,128,128]{2,1,0:T(8,128)(2,1)} %bitcast.16), calls=%async_computation.1 | async-start | bytes 1048576 | tf_op jit(solution)/shard_map/all_to_all | solution.py:72
  139.3 4.8 %fusion.36 = bf16[8,256,8,16]{1,3,2,0:T(8,128)(2,1)S(1)} fusion(bf16[8,8,256,256]{2,3,1,0:T(8,128)(2,1)} %copy-done.2, bf16[8,256,1,8,16]{1,0,4,3,2:T(8,128)(2,1)} %get-tuple-element.20), kind=kOutput, calls=%fused_computation.71 | convolution fusion | flops 134479872 | bytes 9437184 | tf_op jit(solution)/shard_map/jvp(bhqk,bkhd->bqhd)/dot_general | solution.py:27
  144.5 0.9 fusion.82
  145.4 3.3 fusion.63
  148.7 5.0 %all-to-all-done.1 = bf16[16,128,128]{2,1,0:T(8,128)(2,1)} async-done(((bf16[16,128,128]{2,1,0:T(8,128)(2,1)}), bf16[16,128,128]{2,1,0:T(8,128)(2,1)}, u32[]{:S(2)}, u32[]{:S(2)}) %all-to-all-start.1) | async-done | bytes 524320 | tf_op jit(solution)/shard_map/all_to_all | solution.py:72
  153.7 6.4 %scatter_custom_fusion.1 = bf16[2048,128]{1,0:T(8,128)(2,1)S(1)} fusion(s32[2048]{0:T(1024)S(1)} %get-tuple-element.29, bf16[2048,128]{1,0:T(8,128)(2,1)} %bitcast.17, bf16[]{:T(256)} %constant.4.clone.1), kind=kCustom, calls=%fused_computation.102 | custom fusion | bytes 524800 | tf_op jit(solution)/shard_map/scatter | solution.py:79
  160.6 0.9 copy.78
  161.6 9.1 %fusion.11 = (f32[8,8,256]{2,1,0:T(8,128)S(1)}, bf16[8,8,256,256]{2,3,1,0:T(8,128)(2,1)S(1)}) fusion(f32[8,8,256,256]{2,3,1,0:T(8,128)} %get-tuple-element.31, f32[8,8,256]{2,1,0:T(8,128)S(1)} %multiply_divide_fusion, bf16[8,256,1,8,16]{1,0,4,3,2:T(8,128)(2,1)} %copy-done.4, bf16[8,8,16,256]{3,0,2,1:T(8,128)(2,1)} %bitcast.167), kind=kOutput, calls=%fused_computation.19 | convolution fusion | flops 155172864 | bytes 26345472 | tf_op jit(solution)/shard_map/transpose(jvp(bhqk,bkhd->bqhd))/dot_general | solution.py:27
  170.7 8.7 %fusion.32 = bf16[8,256,1,8,16]{1,4,3,0,2:T(8,128)(2,1)} fusion(bf16[8,256,1,8,16]{1,0,4,3,2:T(8,128)(2,1)} %copy-done.14, f32[8,8,256,256]{2,3,1,0:T(8,128)} %get-tuple-element.31, bf16[8,8,256,256]{2,3,1,0:T(8,128)(2,1)S(1)} %get-tuple-element.37, f32[8,8,256]{2,1,0:T(8,128)S(1)} %neg.13, f32[8,8,256]{2,1,0:T(8,128)S(1)} %get-tuple-element.30), kind=kOutput, calls=%fused_computation.67 | convolution fusion | flops 155451392 | bytes 26345472 | tf_op jit(solution)/shard_map/transpose(jvp(bqhd,bkhd->bhqk))/dot_general | solution.py:23
  179.3 8.5 %fusion.31 = bf16[8,256,1,8,16]{1,4,3,0,2:T(8,128)(2,1)} fusion(bf16[8,256,1,8,16]{1,0,4,3,2:T(8,128)(2,1)S(1)} %copy-done.13, f32[8,8,256,256]{2,3,1,0:T(8,128)} %get-tuple-element.31, bf16[8,8,256,256]{2,3,1,0:T(8,128)(2,1)S(1)} %get-tuple-element.37, f32[8,8,256]{2,1,0:T(8,128)S(1)} %neg.13, f32[8,8,256]{2,1,0:T(8,128)S(1)} %get-tuple-element.30), kind=kOutput, calls=%fused_computation.66 | convolution fusion | flops 155451392 | bytes 26345472 | tf_op jit(solution)/shard_map/transpose(jvp(bqhd,bkhd->bhqk))/dot_general | solution.py:23
  188.0 2.3 fusion.35
  190.3 1.3 pad_add_fusion
  191.6 0.9 copy.56
  193.0 1.1 fusion.38
  194.1 1.7 fusion.66
  195.8 0.9 fusion.81
  196.8 32.6 %all-reduce.6 = (f32[128]{0:T(128)}, f32[128]{0:T(128)}) all-reduce(f32[128]{0:T(128)S(1)} %get-tuple-element.10, f32[128]{0:T(128)S(1)} %get-tuple-element.8), channel_id=1, replica_groups=mesh['wide'=16,'grp'=2] {'wide'}, use_global_device_ids=true, to_apply=%region_13.15 | all-reduce | flops 256 | bytes 2048 | tf_op jit(solution)/shard_map/psum | solution.py:81
  229.4 1.4 fusion.44
  230.8 86.6 %all-reduce.10.cloned.1.call-done = (f32[128,384]{1,0:T(8,128)}, f32[128,128]{1,0:T(8,128)}, f32[128,384]{1,0:T(8,128)}, f32[128,128]{1,0:T(8,128)}) async-done(((f32[128,384]{1,0:T(8,128)}, f32[128,128]{1,0:T(8,128)}, f32[128,384]{1,0:T(8,128)}, f32[128,128]{1,0:T(8,128)}), (f32[128,384]{1,0:T(8,128)}, f32[128,128]{1,0:T(8,128)}, f32[128,384]{1,0:T(8,128)}, ...) | async-done | bytes 524304 | tf_op jit(solution)/shard_map/psum | solution.py:81
  317.4 1.6 copy.151
  319.0 1.5 copy.152
  320.5 1.6 copy.153
  322.1 1.5 copy.154
  (89 shorter events, 8.7 us)
Async XLA Ops:
  7.2 64.4 %copy-start = (bf16[128,384]{1,0:T(8,128)(2,1)S(1)}, bf16[128,384]{1,0:T(8,128)(2,1)}, u32[]{:S(2)}) copy-start(bf16[128,384]{1,0:T(8,128)(2,1)} %param.20) | copy-start | bytes 294916
  10.0 0.6 copy-start.22
  10.6 0.6 copy-start.20
  14.3 9.0 %copy-start.14 = (bf16[8,256,1,8,16]{1,0,4,3,2:T(8,128)(2,1)}, bf16[8,256,1,8,16]{1,0,4,3,2:T(8,128)(2,1)S(1)}, u32[]{:S(2)}) copy-start(bf16[8,256,1,8,16]{1,0,4,3,2:T(8,128)(2,1)S(1)} %get-tuple-element.25) | copy-start | bytes 1572868
  14.3 15.9 %copy-start.12 = (bf16[8,256,1,8,16]{1,0,4,3,2:T(8,128)(2,1)}, bf16[8,256,1,8,16]{1,0,4,3,2:T(8,128)(2,1)S(1)}, u32[]{:S(2)}) copy-start(bf16[8,256,1,8,16]{1,0,4,3,2:T(8,128)(2,1)S(1)} %get-tuple-element.24) | copy-start | bytes 1572868
  14.3 20.7 %copy-start.4 = (bf16[8,256,1,8,16]{1,0,4,3,2:T(8,128)(2,1)}, bf16[8,256,1,8,16]{1,0,4,3,2:T(8,128)(2,1)S(1)}, u32[]{:S(2)}) copy-start(bf16[8,256,1,8,16]{1,0,4,3,2:T(8,128)(2,1)S(1)} %get-tuple-element.23) | copy-start | bytes 1572868
  23.3 11.7 %copy-start.3 = (bf16[2048,128]{1,0:T(8,128)(2,1)S(1)}, bf16[2048,128]{1,0:T(8,128)(2,1)}, u32[]{:S(2)}) copy-start(bf16[2048,128]{1,0:T(8,128)(2,1)} %param.12) | copy-start | bytes 1572868
  23.3 11.7 %copy-start.18 = (bf16[128,128]{1,0:T(8,128)(2,1)S(1)}, bf16[128,128]{1,0:T(8,128)(2,1)}, u32[]{:S(2)}) copy-start(bf16[128,128]{1,0:T(8,128)(2,1)} %param.18) | copy-start | bytes 98308
  30.2 3.2 copy-start.1
  30.2 20.1 %copy-start.8 = (bf16[2048,128]{1,0:T(8,128)(2,1)S(1)}, bf16[2048,128]{1,0:T(8,128)(2,1)}, u32[]{:S(2)}) copy-start(bf16[2048,128]{1,0:T(8,128)(2,1)} %param.13) | copy-start | bytes 1572868
  30.2 20.1 %copy-start.24 = (bf16[128,128]{1,0:T(8,128)(2,1)S(1)}, bf16[128,128]{1,0:T(8,128)(2,1)}, u32[]{:S(2)}) copy-start(bf16[128,128]{1,0:T(8,128)(2,1)} %param.21) | copy-start | bytes 98308
  30.2 21.5 %copy-start.25 = (s32[2048]{0:T(1024)S(1)}, s32[2048]{0:T(1024)}, u32[]{:S(2)}) copy-start(s32[2048]{0:T(1024)} %param.15) | copy-start | bytes 24580
  30.2 41.4 %copy-start.27 = (f32[128]{0:T(128)S(1)}, f32[128]{0:T(128)}, u32[]{:S(2)}) copy-start(f32[128]{0:T(128)} %param.19) | copy-start | bytes 1540
  35.0 36.6 %copy-start.6 = (bf16[16,8,8,256]{3,1,2,0:T(8,128)(2,1)}, bf16[16,8,8,256]{3,1,2,0:T(8,128)(2,1)S(1)}, u32[]{:S(2)}) copy-start(bf16[16,8,8,256]{3,1,2,0:T(8,128)(2,1)S(1)} %copy.75) | copy-start | bytes 1572868
  42.7 22.0 %all-to-all-start = ((bf16[16,128,128]{2,1,0:T(8,128)(2,1)}), bf16[16,128,128]{2,1,0:T(8,128)(2,1)S(1)}, u32[]{:S(2)}, u32[]{:S(2)}) async-start(bf16[16,128,128]{2,1,0:T(8,128)(2,1)} %bitcast.173), calls=%async_computation | async-start | bytes 1048576 | tf_op jit(solution)/shard_map/all_to_all | solution.py:64
  76.7 9.0 %copy-start.15 = (bf16[8,256,1,8,16]{1,0,4,3,2:T(8,128)(2,1)}, bf16[8,256,1,8,16]{1,0,4,3,2:T(8,128)(2,1)S(1)}, u32[]{:S(2)}) copy-start(bf16[8,256,1,8,16]{1,0,4,3,2:T(8,128)(2,1)S(1)} %get-tuple-element.22) | copy-start | bytes 1572868
  76.7 9.0 %copy-start.17 = (bf16[8,256,1,8,16]{1,0,4,3,2:T(8,128)(2,1)}, bf16[8,256,1,8,16]{1,0,4,3,2:T(8,128)(2,1)S(1)}, u32[]{:S(2)}) copy-start(bf16[8,256,1,8,16]{1,0,4,3,2:T(8,128)(2,1)S(1)} %get-tuple-element.21) | copy-start | bytes 1572868
  96.7 23.3 %copy-start.2 = (bf16[8,8,256,256]{2,3,1,0:T(8,128)(2,1)}, bf16[8,8,256,256]{2,3,1,0:T(8,128)(2,1)S(1)}, u32[]{:S(2)}) copy-start(bf16[8,8,256,256]{2,3,1,0:T(8,128)(2,1)S(1)} %get-tuple-element.18) | copy-start | bytes 25165828
  97.6 12.2 %copy-start.16 = (bf16[8,256,1,8,16]{1,0,4,3,2:T(8,128)(2,1)S(1)}, bf16[8,256,1,8,16]{1,0,4,3,2:T(8,128)(2,1)}, u32[]{:S(2)}) copy-start(bf16[8,256,1,8,16]{1,0,4,3,2:T(8,128)(2,1)} %copy-done.15) | copy-start | bytes 1572868
  109.8 10.2 %copy-start.10 = (bf16[16,8,8,256]{3,2,1,0:T(8,128)(2,1)S(1)}, bf16[16,8,8,256]{3,2,1,0:T(8,128)(2,1)}, u32[]{:S(2)}) copy-start(bf16[16,8,8,256]{3,2,1,0:T(8,128)(2,1)} %copy.73) | copy-start | bytes 1572868
  122.3 22.2 %copy-start.9 = (bf16[2048,128]{1,0:T(8,128)(2,1)S(1)}, bf16[2048,128]{1,0:T(8,128)(2,1)}, u32[]{:S(2)}) copy-start(bf16[2048,128]{1,0:T(8,128)(2,1)} %param.13) | copy-start | bytes 1572868
  123.8 1.2 copy-start.11
  134.9 18.7 %all-to-all-start.1 = ((bf16[16,128,128]{2,1,0:T(8,128)(2,1)}), bf16[16,128,128]{2,1,0:T(8,128)(2,1)}, u32[]{:S(2)}, u32[]{:S(2)}) async-start(bf16[16,128,128]{2,1,0:T(8,128)(2,1)} %bitcast.16), calls=%async_computation.1 | async-start | bytes 1048576 | tf_op jit(solution)/shard_map/all_to_all | solution.py:72
  139.2 178.2 %all-reduce.10.cloned.1.call-start = ((), (), s32[]{:S(2)}) async-start(), calls=%async_computation.2 | async-start | bytes 1048576 | tf_op jit(solution)/shard_map/psum | solution.py:81
  170.7 8.7 %copy-start.13 = (bf16[8,256,1,8,16]{1,0,4,3,2:T(8,128)(2,1)S(1)}, bf16[8,256,1,8,16]{1,0,4,3,2:T(8,128)(2,1)}, u32[]{:S(2)}) copy-start(bf16[8,256,1,8,16]{1,0,4,3,2:T(8,128)(2,1)} %copy-done.12) | copy-start | bytes 1572868
  170.7 17.2 %slice-start = ((s8[8388608]{0:T(1024)(128)(4,1)}), s8[4194304]{0:T(1024)(128)(4,1)S(1)}, s32[]{:S(2)}) async-start(s8[8388608]{0:T(1024)(128)(4,1)} %bitcast.158), calls=%async_computation.3 | async-start | bytes 8388608
  179.3 8.6 %slice-start.1 = ((s8[8388608]{0:T(1024)(128)(4,1)}), s8[4194304]{0:T(1024)(128)(4,1)S(1)}, s32[]{:S(2)}) async-start(s8[8388608]{0:T(1024)(128)(4,1)} %bitcast.158), calls=%async_computation.4 | async-start | bytes 8388608
  179.3 8.6 %copy-start.5 = (bf16[16,8,8,256]{3,2,1,0:T(8,128)(2,1)S(1)}, bf16[16,8,8,256]{3,2,1,0:T(8,128)(2,1)}, u32[]{:S(2)}) copy-start(bf16[16,8,8,256]{3,2,1,0:T(8,128)(2,1)} %copy.78) | copy-start | bytes 1572868
  187.9 5.1 %copy-start.19 = (bf16[128,384]{1,0:T(8,128)(2,1)S(1)}, bf16[128,384]{1,0:T(8,128)(2,1)}, u32[]{:S(2)}) copy-start(bf16[128,384]{1,0:T(8,128)(2,1)} %param.17) | copy-start | bytes 294916
  187.9 5.1 %copy-start.21 = (f32[2048]{0:T(1024)S(1)}, f32[2048]{0:T(1024)}, u32[]{:S(2)}) copy-start(f32[2048]{0:T(1024)} %copy-done.20) | copy-start | bytes 24580
  187.9 5.1 %copy-start.26 = (f32[128]{0:T(128)S(1)}, f32[128]{0:T(128)}, u32[]{:S(2)}) copy-start(f32[128]{0:T(128)} %param.16) | copy-start | bytes 1540
  188.0 7.9 %copy-start.7 = (bf16[16,8,8,256]{3,1,2,0:T(8,128)(2,1)S(1)}, bf16[16,8,8,256]{3,1,2,0:T(8,128)(2,1)}, u32[]{:S(2)}) copy-start(bf16[16,8,8,256]{3,1,2,0:T(8,128)(2,1)} %copy-done.6) | copy-start | bytes 1572868
  188.0 8.8 %copy-start.23 = (f32[2048]{0:T(1024)S(1)}, f32[2048]{0:T(1024)}, u32[]{:S(2)}) copy-start(f32[2048]{0:T(1024)} %copy-done.22) | copy-start | bytes 24580
Sparse Core Ops, SparseCore 0:
  229.5 87.8 all-reduce.9
where the time goes:
time: 337 us; the launch traced here: 331 us
  waiting for transfers between devices  105 us (31%)
  matrix products  102 us (30%)
  local copies, waits for them, and re-layouts  41 us (12%)
  blocking collectives  32.6 us (10%)
  other arithmetic  23.8 us (7%)
  between operations  15.1 us (4%)
  starting transfers between devices  11.9 us (4%)
    psum x1, waiting for transfers between devices, body(): lax.psum((d_gain_a, d_qkv_a, d_proj_a, d_gain_b, d_qkv_b, d_proj_b), 'wide')  86.6 us
    dot_general x4, matrix products, ball_core(): jnp.einsum('bqhd,bkhd->bhqk', query, keys, preferred_element_type=jnp.flo...  39.6 us
    psum x1, blocking collectives, body(): lax.psum((d_gain_a, d_qkv_a, d_proj_a, d_gain_b, d_qkv_b, d_proj_b), 'wide')  32.6 us
    dot_general x6, matrix products, ball_core(): jnp.einsum('bhqk,bkhd->bqhd', weights, values, preferred_element_type=jnp...  30.5 us
    sub x2, matrix products, ball_core(): weights = jax.nn.softmax(scores, axis=-1).astype(jnp.bfloat16)  17.9 us
    unnamed x72, local copies, waits for them, and re-layouts  15.8 us
    all_to_all x1, waiting for transfers between devices, body(): lax.all_to_all(outgoing, 'wide', split_axis=0, concat_axis=0, tiled=True)  12.9 us
    scatter x1, other arithmetic, body(): jnp.zeros((rows, width), jnp.bfloat16).at[order_recv].set(d_rotated)  8.47 us
  transfers between devices with their start and end apart: 3, of which 3 were waited for; matrix products, arithmetic and copies ran while one was open for 4% of the time, Pallas kernels for 0%

commit v1 on v0

v1 whole, which is shorter than its diff:
```python
import functools

import jax
import jax.numpy as jnp
from jax import lax
from jax.experimental import pallas as pl
from jax.experimental.pallas import tpu as pltpu
from jax.sharding import PartitionSpec as P

D = 128
HEADS = 8
BALL = 256
HEAD_DIM = 16
EPS = 1e-06
LOG2E = 1.4426950408889634
LN2 = 0.6931471805599453
SCALE = HEAD_DIM ** (-0.5)
VMEM_LIMIT = 56 * 1024 * 1024
UNROLL = 32
GRAD_ROWS = 4 * D + 32

f32 = jnp.float32
bf16 = jnp.bfloat16


def dot(a, b, ca=1, cb=0):
    return lax.dot_general(a, b, (((ca,), (cb,)), ((), ())), preferred_element_type=f32)


def head_mask(h):
    lane = lax.broadcasted_iota(jnp.int32, (1, D), 1)
    return jnp.where(lane // HEAD_DIM == h, 1.0, 0.0).astype(bf16)


def rows_of(h):
    return slice(h * HEAD_DIM, (h + 1) * HEAD_DIM)


def inverse_rms(values):
    return lax.rsqrt(jnp.mean(values * values, axis=-1, keepdims=True) + EPS)


def project(normed, w_ref, wt_ref):
    qkv_t = dot(wt_ref[...], normed, 1, 1)
    q_t = (qkv_t[:D] * (SCALE * LOG2E)).astype(bf16)
    k_t = qkv_t[D : 2 * D].astype(bf16)
    v_t = qkv_t[2 * D :].astype(bf16)
    kv = dot(normed, w_ref[:, D:]).astype(bf16)
    return q_t, k_t, v_t, kv[:, :D], kv[:, D:]


def forward_head(h, k_rows, q_t, v_t):
    scores = dot(k_rows * head_mask(h), q_t)
    top = jnp.max(scores, axis=0, keepdims=True)
    weights = jnp.exp2(scores - top).astype(bf16)
    ones = jnp.ones((HEAD_DIM, BALL), bf16)
    summed = dot(jnp.concatenate([v_t[rows_of(h)], ones], axis=0), weights)
    inv = 1.0 / summed[HEAD_DIM : HEAD_DIM + 1]
    return weights, inv, (summed[:HEAD_DIM] * inv).astype(bf16)


def backward_head(h, weights, att_t, d_att_t, q_t, k_t, v_rows, d_qkv_t_ref):
    rows = rows_of(h)
    own = d_att_t[rows]
    delta = jnp.sum(own.astype(f32) * att_t[rows].astype(f32), axis=0, keepdims=True)
    d_weights = dot(v_rows * head_mask(h), d_att_t)
    d_scores = (weights.astype(f32) * (d_weights - delta)).astype(bf16)
    d_qkv_t_ref[h * HEAD_DIM : (h + 1) * HEAD_DIM, :] = (dot(k_t[rows], d_scores) * SCALE).astype(bf16)
    d_qkv_t_ref[D + h * HEAD_DIM : D + (h + 1) * HEAD_DIM, :] = (dot(q_t[rows], d_scores, 1, 1) * LN2).astype(bf16)
    d_qkv_t_ref[2 * D + h * HEAD_DIM : 2 * D + (h + 1) * HEAD_DIM, :] = dot(own, weights, 1, 1).astype(bf16)


def backward_rows(values, inv_rms, gain, normed, w_ref, d_out, att_t, d_qkv_t, grads_ref):
    grads_ref[: 3 * D, :] += dot(d_qkv_t, normed)
    grads_ref[3 * D : 4 * D, :] += dot(att_t, d_out)
    d_normed = dot(w_ref[...], d_qkv_t).T
    unit = values * inv_rms
    grads_ref[4 * D : 4 * D + 1, :] += jnp.sum(d_normed * unit, axis=0, keepdims=True)
    d_unit = d_normed * gain
    along = jnp.mean(d_unit * unit, axis=-1, keepdims=True)
    return d_out.astype(f32) + inv_rms * (d_unit - unit * along)


def for_rows(count, copy_row):
    def step(i, carry):
        for j in range(UNROLL):
            copy_row(i * UNROLL + j)
        return carry

    lax.fori_loop(0, count // UNROLL, step, 0)


def first_kernel(order_ref, x_ref, gain_ref, w_ref, proj_ref, sent_ref, e_ref, inv_ref, att_ref, q_ref, k_ref, v_ref, wt, out, picked):
    ball = pl.program_id(0)

    @pl.when(ball == 0)
    def _():
        wt[...] = w_ref[...].T

    values = x_ref[...].astype(f32)
    normed = (values * inverse_rms(values) * gain_ref[...]).astype(bf16)
    q_t, k_t, v_t, k_rows, v_rows = project(normed, w_ref, wt)
    q_ref[0] = q_t
    k_ref[0] = k_t
    v_ref[...] = v_rows
    for h in range(HEADS):
        weights, inv, att = forward_head(h, k_rows, q_t, v_t)
        e_ref[0, h] = weights
        inv_ref[0, h : h + 1, :] = inv
        att_ref[0, rows_of(h), :] = att
    rows = values + dot(att_ref[0], proj_ref[...], 0, 0)
    out[pl.ds(pl.multiple_of(ball * BALL, BALL), BALL), :] = rows

    @pl.when(ball == pl.num_programs(0) - 1)
    def _():
        def pick(r):
            picked[pl.ds(r, 1), :] = out[pl.ds(order_ref[r], 1), :]

        for_rows(picked.shape[0], pick)
        sent_ref[...] = picked[...].astype(bf16)


def second_kernel(order_ref, came_ref, d_out_ref, gain_ref, w_ref, proj_ref, sent_ref, grads_ref, wt, came, placed, e_s, inv_s, att_s, d_qkv_t, d_in, d_came):
    ball = pl.program_id(0)

    @pl.when(ball == 0)
    def _():
        wt[...] = w_ref[...].T
        came[...] = came_ref[...].astype(f32)
        grads_ref[...] = jnp.zeros_like(grads_ref)

    base = ball * BALL

    def pick(r):
        placed[pl.ds(r, 1), :] = came[pl.ds(order_ref[base + r], 1), :]

    for_rows(BALL, pick)
    values = placed[...]
    inv_rms = inverse_rms(values)
    gain = gain_ref[...]
    normed = (values * inv_rms * gain).astype(bf16)
    q_t, k_t, v_t, k_rows, v_rows = project(normed, w_ref, wt)
    for h in range(HEADS):
        weights, inv, att = forward_head(h, k_rows, q_t, v_t)
        e_s[h] = weights
        inv_s[rows_of(h), :] = jnp.broadcast_to(inv, (HEAD_DIM, BALL))
        att_s[rows_of(h), :] = att
    d_out = d_out_ref[...]
    d_att_t = (dot(proj_ref[...], d_out, 1, 1) * inv_s[...]).astype(bf16)
    att_t = att_s[...]
    for h in range(HEADS):
        backward_head(h, e_s[h], att_t, d_att_t, q_t, k_t, v_rows, d_qkv_t)
    d_in[...] = backward_rows(values, inv_rms, gain, normed, w_ref, d_out, att_t, d_qkv_t[...], grads_ref)

    def put(r):
        d_came[pl.ds(order_ref[base + r], 1), :] = d_in[pl.ds(r, 1), :]

    for_rows(BALL, put)

    @pl.when(ball == pl.num_programs(0) - 1)
    def _():
        sent_ref[...] = d_came[...].astype(bf16)


def third_kernel(order_ref, came_ref, x_ref, gain_ref, w_ref, proj_ref, e_ref, inv_ref, att_ref, q_ref, k_ref, v_ref, d_x_ref, grads_ref, came, d_first, d_qkv_t):
    ball = pl.program_id(0)

    @pl.when(ball == 0)
    def _():
        came[...] = came_ref[...].astype(f32)
        grads_ref[...] = jnp.zeros_like(grads_ref)

        def put(r):
            d_first[pl.ds(order_ref[r], 1), :] = came[pl.ds(r, 1), :]

        for_rows(came.shape[0], put)

    values = x_ref[...].astype(f32)
    inv_rms = inverse_rms(values)
    gain = gain_ref[...]
    normed = (values * inv_rms * gain).astype(bf16)
    d_out = d_first[pl.ds(pl.multiple_of(ball * BALL, BALL), BALL), :].astype(bf16)
    d_att = dot(proj_ref[...], d_out, 1, 1)
    att_t, q_t, k_t, v_rows = att_ref[0], q_ref[0], k_ref[0], v_ref[...]
    d_att_t = jnp.concatenate([d_att[rows_of(h)] * inv_ref[0, h : h + 1, :] for h in range(HEADS)], axis=0).astype(bf16)
    for h in range(HEADS):
        backward_head(h, e_ref[0, h], att_t, d_att_t, q_t, k_t, v_rows, d_qkv_t)
    d_x = backward_rows(values, inv_rms, gain, normed, w_ref, d_out, att_t, d_qkv_t[...], grads_ref)
    d_x_ref[...] = d_x.astype(bf16)


def whole(shape):
    return pl.BlockSpec(shape, lambda i: (0,) * len(shape))


ORDER = pl.BlockSpec(memory_space=pltpu.SMEM)
BALL_ROWS = pl.BlockSpec((BALL, D), lambda i: (i, 0))
BALL_COLS = pl.BlockSpec((1, D, BALL), lambda i: (i, 0, 0))
BALL_STATS = pl.BlockSpec((1, HEADS, BALL), lambda i: (i, 0, 0))
BALL_WEIGHTS = pl.BlockSpec((1, HEADS, BALL, BALL), lambda i: (i, 0, 0, 0))
PARAMS = [whole((1, D)), whole((D, 3 * D)), whole((D, D))]


def call(kernel, grid, in_specs, outs, scratch):
    return pl.pallas_call(
        kernel,
        grid=(grid,),
        in_specs=in_specs,
        out_specs=[spec for spec, _, _ in outs],
        out_shape=[jax.ShapeDtypeStruct(shape, kind) for _, shape, kind in outs],
        scratch_shapes=[pltpu.VMEM(shape, kind) for shape, kind in scratch],
        compiler_params=pltpu.CompilerParams(vmem_limit_bytes=VMEM_LIMIT),
    )


def first_call(order, x, gain, w, proj):
    rows = x.shape[0]
    balls = rows // BALL
    return call(
        first_kernel,
        balls,
        [ORDER, BALL_ROWS] + PARAMS,
        [
            (whole((rows, D)), (rows, D), bf16),
            (BALL_WEIGHTS, (balls, HEADS, BALL, BALL), bf16),
            (BALL_STATS, (balls, HEADS, BALL), f32),
            (BALL_COLS, (balls, D, BALL), bf16),
            (BALL_COLS, (balls, D, BALL), bf16),
            (BALL_COLS, (balls, D, BALL), bf16),
            (BALL_ROWS, (rows, D), bf16),
        ],
        [((3 * D, D), bf16), ((rows, D), f32), ((rows, D), f32)],
    )(order, x, gain, w, proj)


def second_call(order, came, d_out, gain, w, proj):
    rows = came.shape[0]
    return call(
        second_kernel,
        rows // BALL,
        [ORDER, whole((rows, D)), BALL_ROWS] + PARAMS,
        [(whole((rows, D)), (rows, D), bf16), (whole((GRAD_ROWS, D)), (GRAD_ROWS, D), f32)],
        [
            ((3 * D, D), bf16),
            ((rows, D), f32),
            ((BALL, D), f32),
            ((HEADS, BALL, BALL), bf16),
            ((D, BALL), f32),
            ((D, BALL), bf16),
            ((3 * D, BALL), bf16),
            ((BALL, D), f32),
            ((rows, D), f32),
        ],
    )(order, came, d_out, gain, w, proj)


def third_call(order, came, x, gain, w, proj, kept):
    rows = came.shape[0]
    return call(
        third_kernel,
        rows // BALL,
        [ORDER, whole((rows, D)), BALL_ROWS] + PARAMS + [BALL_WEIGHTS, BALL_STATS, BALL_COLS, BALL_COLS, BALL_COLS, BALL_ROWS],
        [(BALL_ROWS, (rows, D), bf16), (whole((GRAD_ROWS, D)), (GRAD_ROWS, D), f32)],
        [((rows, D), f32), ((rows, D), f32), ((3 * D, BALL), bf16)],
    )(order, came, x, gain, w, proj, *kept)


def exchange(rows):
    return lax.all_to_all(rows, "wide", split_axis=0, concat_axis=0, tiled=True)


def swap(part, peers, apart):
    return lax.ppermute(part, "wide", [(i, i ^ apart) for i in range(peers)])


def sum_over_wide(part):
    peers = lax.axis_size("wide")
    half = part.shape[0] // 2
    core = lax.axis_index("wide") % 2
    part = part.astype(bf16)
    low, high = part[:half], part[half:]
    mine = jnp.where(core == 0, low, high)
    other = jnp.where(core == 0, high, low)
    total = mine.astype(f32) + swap(other, peers, 1).astype(f32)
    apart = 2
    while apart < peers:
        sent = total.astype(bf16)
        total = sent.astype(f32) + swap(sent, peers, apart).astype(f32)
        apart *= 2
    mine = total.astype(bf16)
    other = swap(mine, peers, 1)
    low = jnp.where(core == 0, mine, other)
    high = jnp.where(core == 0, other, mine)
    return jnp.concatenate([low, high], axis=0).astype(f32)


def body(tokens, cotangent, order_send, order_recv, gain_a, qkv_a, proj_a, gain_b, qkv_b, proj_b):
    gain_a = gain_a.reshape(1, D)
    gain_b = gain_b.reshape(1, D)
    sent, *kept = first_call(order_send, tokens, gain_a, qkv_a, proj_a)
    d_sent, grads_b = second_call(order_recv, exchange(sent), cotangent, gain_b, qkv_b, proj_b)
    d_tokens, grads_a = third_call(order_send, exchange(d_sent), tokens, gain_a, qkv_a, proj_a, kept)
    total = sum_over_wide(jnp.concatenate([grads_a, grads_b], axis=0))
    outs = [d_tokens]
    for start in (0, GRAD_ROWS):
        outs.append(total[start + 4 * D])
        outs.append(total[start : start + 3 * D].T)
        outs.append(total[start + 3 * D : start + 4 * D])
    return tuple(outs)


def solution(mesh):
    rows = P(("grp", "wide"), None)
    order = P(("grp", "wide"))
    return jax.shard_map(
        body,
        mesh=mesh,
        in_specs=(rows, rows, order, order) + (P(),) * 6,
        out_specs=(rows,) + (P("grp"), P("grp", None), P("grp", None)) * 2,
        check_vma=False,
    )
```

time: 337 us -> 163 us (0.48); the launches traced: 331 us -> 163 us
  matrix products: 102 us -> 0 us
  Pallas kernels: 0 us -> 94.3 us
  waiting for transfers between devices: 105 us -> 31 us
  local copies, waits for them, and re-layouts: 41 us -> 2.45 us
  other arithmetic: 23.8 us -> 3.35 us
  between operations: 15.1 us -> 0.71 us
  blocking collectives: 32.6 us -> 22 us
    pallas_call x0 -> x3, Pallas kernels: none -> 94.3 us  [the longest x1 44.2 us: second_call(): call(second_kernel, rows // BALL, [ORDER, whole((rows, D)), BALL_ROWS] +...]
    psum x1 -> x0, waiting for transfers between devices: 86.6 us -> none  [body(): lax.psum((d_gain_a, d_qkv_a, d_proj_a, d_gain_b, d_qkv_b, d_proj_b), 'wide')]
    dot_general x21 -> x0, matrix products: 84.1 us -> none  [the longest x4 39.6 us: ball_core(): jnp.einsum('bqhd,bkhd->bhqk', query, keys, preferred_element_type=jnp.flo...]
    psum x1 -> x0, blocking collectives: 32.6 us -> none  [body(): lax.psum((d_gain_a, d_qkv_a, d_proj_a, d_gain_b, d_qkv_b, d_proj_b), 'wide')]
    all_to_all x0 -> x1, blocking collectives: none -> 22 us  [exchange(): return lax.all_to_all(rows, 'wide', split_axis=0, concat_axis=0, tiled=True)]
    sub x2 -> x0, matrix products: 17.9 us -> none  [ball_core(): weights = jax.nn.softmax(scores, axis=-1).astype(jnp.bfloat16)]
    ppermute x0 -> x5, waiting for transfers between devices: none -> 16.5 us  [swap(): return lax.ppermute(part, 'wide', [(i, i ^ apart) for i in range(peers)])]
    unnamed x72 -> x6, local copies, waits for them, and re-layouts: 15.8 us -> 2.42 us
  transfers between devices with their start and end apart: 3 -> 6, of which waited for: 3 -> 6; matrix products, arithmetic and copies ran while one was open for 4% -> 0% of each run, Pallas kernels for 0% -> 0%
where the time goes in v1:
time: 163 us
  Pallas kernels  94.3 us (58%)
  waiting for transfers between devices  31 us (19%)
  blocking collectives  22 us (13%)
  starting transfers between devices  9.26 us (6%)
  other arithmetic  3.35 us (2%)
  local copies, waits for them, and re-layouts  2.45 us (2%)
    pallas_call x1, Pallas kernels, second_call(): call(second_kernel, rows // BALL, [ORDER, whole((rows, D)), BALL_ROWS] +...  44.2 us
    pallas_call x1, Pallas kernels, first_call(): call(first_kernel, balls, [ORDER, BALL_ROWS] + PARAMS, [(whole((rows, D))...  26.3 us
    pallas_call x1, Pallas kernels, third_call(): call(third_kernel, rows // BALL, [ORDER, whole((rows, D)), BALL_ROWS] + P...  23.8 us
    all_to_all x1, blocking collectives, exchange(): return lax.all_to_all(rows, 'wide', split_axis=0, concat_axis=0, tiled=True)  22 us
    ppermute x5, waiting for transfers between devices, swap(): return lax.ppermute(part, 'wide', [(i, i ^ apart) for i in range(peers)])  16.5 us
    all_to_all x1, waiting for transfers between devices, exchange(): return lax.all_to_all(rows, 'wide', split_axis=0, concat_axis=0, tiled=True)  14.5 us
    ppermute x5, starting transfers between devices, swap(): return lax.ppermute(part, 'wide', [(i, i ^ apart) for i in range(peers)])  5.02 us
    all_to_all x1, starting transfers between devices, exchange(): return lax.all_to_all(rows, 'wide', split_axis=0, concat_axis=0, tiled=True)  4.24 us
  transfers between devices with their start and end apart: 6, of which 6 were waited for; matrix products, arithmetic and copies ran while one was open for 0% of the time, Pallas kernels for 0%

profile of v1, /device:TPU:0, one launch (start us, length us, event | category | flops | bytes accessed | tf_op | source)
XLA Modules:
  0.0 163.0 jit_solution(4664751778576821219)
XLA Ops:
  0.6 26.3 %shard_map.153 = (bf16[2048,128]{1,0:T(8,128)(2,1)}, bf16[8,8,256,256]{3,2,1,0:T(8,128)(2,1)}, f32[8,8,256]{2,1,0:T(8,128)}, bf16[8,128,256]{2,1,0:T(8,128)(2,1)...) custom-call(s32[2048]{0:T(1024)} %order_ref.5, bf16[2048,128]{1,0:T(8,128)(2,1)} %x_ref.3, ...), custom_call_target="tpu_custom_call" | custom-call | tf_op jit(solution)/shard_map/pallas_call | solution.py:219
  26.9 22.0 %all_to_all.22 = bf16[16,128,128]{2,1,0:T(8,128)(2,1)} all-to-all(bf16[16,128,128]{2,1,0:T(8,128)(2,1)} %bitcast.17), channel_id=1, replica_groups=mesh['wide'=16,'grp'=2] {'wide'}, dimensions={0} | all-to-all | bytes 1048576 | tf_op jit(solution)/shard_map/all_to_all | solution.py:269
  48.9 44.2 %shard_map.154 = (bf16[2048,128]{1,0:T(8,128)(2,1)}, f32[544,128]{1,0:T(8,128)}) custom-call(s32[2048]{0:T(1024)} %order_ref.4, bf16[2048,128]{1,0:T(8,128)(2,1)} %bitcast.15, bf16[2048,128]{1,0:T(8,128)(2,1)} %d_out_ref.1, f32[1,128]{1,0:T(1,128)} %bitcast.20, bf16[128,384]{1,0:T(8,128)(2,1)} %w_ref.4, bf16[128,128]{1,0:T(8,128)(2,1)} %proj_ref.4), custom_call_target="tpu_custom_call" | custom-call | tf_op jit(solution)/shard_map/pallas_call | solution.py:238
  93.1 0.0 copy-start.1
  93.1 4.2 %all-to-all-start.1 = ((bf16[16,128,128]{2,1,0:T(8,128)(2,1)}), bf16[16,128,128]{2,1,0:T(8,128)(2,1)S(1)}, u32[]{:S(2)}, u32[]{:S(2)}) async-start(bf16[16,128,128]{2,1,0:T(8,128)(2,1)} %bitcast.16), calls=%async_computation.1 | async-start | bytes 1048576 | tf_op jit(solution)/shard_map/all_to_all | solution.py:269
  97.4 14.5 %all-to-all-done.1 = bf16[16,128,128]{2,1,0:T(8,128)(2,1)S(1)} async-done(((bf16[16,128,128]{2,1,0:T(8,128)(2,1)}), bf16[16,128,128]{2,1,0:T(8,128)(2,1)S(1)}, u32[]{:S(2)}, u32[]{:S(2)}) %all-to-all-start.1) | async-done | bytes 524320 | tf_op jit(solution)/shard_map/all_to_all | solution.py:269
  111.8 0.0 copy-start
  111.8 0.8 copy-done
  112.6 23.8 %shard_map.155 = (bf16[2048,128]{1,0:T(8,128)(2,1)}, f32[544,128]{1,0:T(8,128)}) custom-call(s32[2048]{0:T(1024)} %order_ref.5, bf16[2048,128]{1,0:T(8,128)(2,1)} %bitcast.14, bf16[2048,128]{1,0:T(8,128)(2,1)} %x_ref.3, f32[1,128]{1,0:T(1,128)} %bitcast.19, bf16[128,384]{1,0:T(8,128)(2,1)} %w_ref.5, bf16[128,128]{1,0:T(8,128)(2,1)} %proj_ref.5, ...), custom_call_target="tpu_custom_call" | custom-call | tf_op jit(solution)/shard_map/pallas_call | solution.py:259
  136.4 0.0 copy-done.1
  136.4 1.0 broadcast_select_fusion.2
  137.4 0.1 collective-permute-start
  137.5 1.3 collective-permute-done
  138.8 1.0 add_convert_fusion.3
  139.8 0.9 collective-permute-start.1
  140.7 4.9 %collective-permute-done.1 = bf16[544,128]{1,0:T(8,128)(2,1)S(1)} collective-permute-done((bf16[544,128]{1,0:T(8,128)(2,1)S(1)}, bf16[544,128]{1,0:T(8,128)(2,1)S(1)}, u32[]{:S(2)}, u32[]{:S(2)}) %collective-permute-start.1) | collective-permute-done | bytes 139296 | tf_op jit(solution)/shard_map/ppermute | solution.py:273
  145.7 1.7 %collective-permute-start.2 = (bf16[544,128]{1,0:T(8,128)(2,1)S(1)}, bf16[544,128]{1,0:T(8,128)(2,1)S(1)}, u32[]{:S(2)}, u32[]{:S(2)}) collective-permute-start(bf16[544,128]{1,0:T(8,128)(2,1)S(1)} %add_convert_fusion.2), channel_id=1, source_target_pairs={{0,8},{2,10},{4,12},{6,14},{8,0},{10,2},{12,4},{14,6},{16,24},{18,... | collective-permute-start | bytes 417800 | tf_op jit(solution)/shard_map/ppermute | solution.py:273
  147.3 3.5 %collective-permute-done.2 = bf16[544,128]{1,0:T(8,128)(2,1)S(1)} collective-permute-done((bf16[544,128]{1,0:T(8,128)(2,1)S(1)}, bf16[544,128]{1,0:T(8,128)(2,1)S(1)}, u32[]{:S(2)}, u32[]{:S(2)}) %collective-permute-start.2) | collective-permute-done | bytes 139296 | tf_op jit(solution)/shard_map/ppermute | solution.py:273
  150.8 2.3 %collective-permute-start.3 = (bf16[544,128]{1,0:T(8,128)(2,1)S(1)}, bf16[544,128]{1,0:T(8,128)(2,1)S(1)}, u32[]{:S(2)}, u32[]{:S(2)}) collective-permute-start(bf16[544,128]{1,0:T(8,128)(2,1)S(1)} %add_convert_fusion.1), channel_id=1, source_target_pairs={{0,16},{2,18},{4,20},{6,22},{8,24},{10,26},{12,28},{14,30},{16,0},... | collective-permute-start | bytes 417800 | tf_op jit(solution)/shard_map/ppermute | solution.py:273
  153.2 5.5 %collective-permute-done.3 = bf16[544,128]{1,0:T(8,128)(2,1)S(1)} collective-permute-done((bf16[544,128]{1,0:T(8,128)(2,1)S(1)}, bf16[544,128]{1,0:T(8,128)(2,1)S(1)}, u32[]{:S(2)}, u32[]{:S(2)}) %collective-permute-start.3) | collective-permute-done | bytes 139296 | tf_op jit(solution)/shard_map/ppermute | solution.py:273
  158.7 0.1 collective-permute-start.4
  158.7 1.3 collective-permute-done.4
  160.1 0.5 convert_bitcast_fusion
  160.7 0.7 maximum_convert_fusion.1
  161.4 0.8 copy.17
  162.2 0.8 copy.18
  (6 shorter events, 0.2 us)
Async XLA Ops:
  93.1 43.3 %copy-start.1 = (f32[544,128]{1,0:T(8,128)S(1)}, f32[544,128]{1,0:T(8,128)}, u32[]{:S(2)}) copy-start(f32[544,128]{1,0:T(8,128)} %get-tuple-element.28) | copy-start | bytes 835588
  93.1 18.7 %all-to-all-start.1 = ((bf16[16,128,128]{2,1,0:T(8,128)(2,1)}), bf16[16,128,128]{2,1,0:T(8,128)(2,1)S(1)}, u32[]{:S(2)}, u32[]{:S(2)}) async-start(bf16[16,128,128]{2,1,0:T(8,128)(2,1)} %bitcast.16), calls=%async_computation.1 | async-start | bytes 1048576 | tf_op jit(solution)/shard_map/all_to_all | solution.py:269
  111.8 0.8 copy-start
  137.4 1.4 collective-permute-start
  139.8 5.8 %collective-permute-start.1 = (bf16[544,128]{1,0:T(8,128)(2,1)S(1)}, bf16[544,128]{1,0:T(8,128)(2,1)S(1)}, u32[]{:S(2)}, u32[]{:S(2)}) collective-permute-start(bf16[544,128]{1,0:T(8,128)(2,1)S(1)} %add_convert_fusion.3), channel_id=1, source_target_pairs={{0,4},{2,6},{4,0},{6,2},{8,12},{10,14},{12,8},{14,10},{16,20},{18,... | collective-permute-start | bytes 417800 | tf_op jit(solution)/shard_map/ppermute | solution.py:273
  145.7 5.1 %collective-permute-start.2 = (bf16[544,128]{1,0:T(8,128)(2,1)S(1)}, bf16[544,128]{1,0:T(8,128)(2,1)S(1)}, u32[]{:S(2)}, u32[]{:S(2)}) collective-permute-start(bf16[544,128]{1,0:T(8,128)(2,1)S(1)} %add_convert_fusion.2), channel_id=1, source_target_pairs={{0,8},{2,10},{4,12},{6,14},{8,0},{10,2},{12,4},{14,6},{16,24},{18,... | collective-permute-start | bytes 417800 | tf_op jit(solution)/shard_map/ppermute | solution.py:273
  150.8 7.8 %collective-permute-start.3 = (bf16[544,128]{1,0:T(8,128)(2,1)S(1)}, bf16[544,128]{1,0:T(8,128)(2,1)S(1)}, u32[]{:S(2)}, u32[]{:S(2)}) collective-permute-start(bf16[544,128]{1,0:T(8,128)(2,1)S(1)} %add_convert_fusion.1), channel_id=1, source_target_pairs={{0,16},{2,18},{4,20},{6,22},{8,24},{10,26},{12,28},{14,30},{16,0},... | collective-permute-start | bytes 417800 | tf_op jit(solution)/shard_map/ppermute | solution.py:273
  158.7 1.4 collective-permute-start.4

commit v2 on v0

v2 whole, which is shorter than its diff:
```python
import jax
import jax.numpy as jnp
from jax import lax
from jax.experimental import pallas as pl
from jax.experimental.pallas import tpu as pltpu
from jax.sharding import PartitionSpec as P

D = 128
HEADS = 8
BALL = 256
HEAD_DIM = 16
EPS = 1e-06
LOG2E = 1.4426950408889634
LN2 = 0.6931471805599453
SCALE = HEAD_DIM ** (-0.5)
VMEM_LIMIT = 56 * 1024 * 1024
CHUNK = BALL // HEADS
GRAD_HALF = 2 * D + 16

f32 = jnp.float32
bf16 = jnp.bfloat16


def dot(a, b, ca=1, cb=0):
    return lax.dot_general(a, b, (((ca,), (cb,)), ((), ())), preferred_element_type=f32)


def head_mask(h):
    lane = lax.broadcasted_iota(jnp.int32, (1, D), 1)
    return jnp.where(lane // HEAD_DIM == h, 1.0, 0.0).astype(bf16)


def rows_of(h):
    return slice(h * HEAD_DIM, (h + 1) * HEAD_DIM)


def inverse_rms(values):
    return lax.rsqrt(jnp.mean(values * values, axis=-1, keepdims=True) + EPS)


def staggered(count, *stages):
    last = max(lag for lag, _ in stages)
    for step in range(count + last):
        for lag, stage in stages:
            if 0 <= step - lag < count:
                stage(step - lag)


def at_first(stage):
    return lambda i: stage(i // HEADS) if i % HEADS == 0 else None


def at_last(stage):
    return lambda i: stage(i // HEADS) if i % HEADS == HEADS - 1 else None


def ball_rows(ball):
    return slice(ball * BALL, (ball + 1) * BALL)


def project(normed, w_ref, wt_ref):
    qkv_t = dot(wt_ref[...], normed, 1, 1)
    q_t = (qkv_t[:D] * (SCALE * LOG2E)).astype(bf16)
    k_t = qkv_t[D : 2 * D].astype(bf16)
    v_t = qkv_t[2 * D :].astype(bf16)
    kv = dot(normed, w_ref[:, D:]).astype(bf16)
    return q_t, k_t, v_t, kv[:, :D], kv[:, D:]


class Forward:
    def __init__(self, e_ref, inv_ref, att_ref):
        self.e_ref, self.inv_ref, self.att_ref = e_ref, inv_ref, att_ref
        self.parts, self.scores = {}, {}

    def score(self, i):
        ball, h = divmod(i, HEADS)
        q_t, _, _, k_rows, _ = self.parts[ball]
        self.scores[i] = dot(k_rows * head_mask(h), q_t)

    def soften(self, i):
        ball, h = divmod(i, HEADS)
        own = self.scores.pop(i)
        self.e_ref[ball, h] = jnp.exp2(own - jnp.max(own, axis=0, keepdims=True)).astype(bf16)

    def attend(self, i):
        ball, h = divmod(i, HEADS)
        ones = jnp.ones((HEAD_DIM, BALL), bf16)
        stacked = jnp.concatenate([self.parts[ball][2][rows_of(h)], ones], axis=0)
        summed = dot(stacked, self.e_ref[ball, h])
        inv = 1.0 / summed[HEAD_DIM : HEAD_DIM + 1]
        self.inv_ref[ball, h : h + 1, :] = inv
        self.att_ref[ball, rows_of(h), :] = (summed[:HEAD_DIM] * inv).astype(bf16)


class Backward:
    def __init__(self, e_ref, inv_ref, att_ref, d_s, d_qkv_t, w_ref, proj_ref, gain_ref, sums):
        self.e_ref, self.inv_ref, self.att_ref, self.d_s, self.d_qkv_t = e_ref, inv_ref, att_ref, d_s, d_qkv_t
        self.w_ref, self.proj_ref, self.gain_ref, self.sums = w_ref, proj_ref, gain_ref, sums
        self.parts, self.rows, self.d_out, self.d_att, self.d_weights = {}, {}, {}, {}, {}

    def join(self, ball, d_out):
        inv = [jnp.broadcast_to(self.inv_ref[ball, h : h + 1, :], (HEAD_DIM, BALL)) for h in range(HEADS)]
        self.d_out[ball] = d_out
        self.d_att[ball] = (dot(self.proj_ref[...], d_out, 1, 1) * jnp.concatenate(inv, axis=0)).astype(bf16)

    def weigh(self, i):
        ball, h = divmod(i, HEADS)
        self.d_weights[i] = dot(self.parts[ball][2] * head_mask(h), self.d_att[ball])

    def score(self, i):
        ball, h = divmod(i, HEADS)
        own = self.d_att[ball][rows_of(h)]
        att = self.att_ref[ball, rows_of(h), :]
        delta = jnp.sum(own.astype(f32) * att.astype(f32), axis=0, keepdims=True)
        self.d_s[ball, h] = (self.e_ref[ball, h].astype(f32) * (self.d_weights.pop(i) - delta)).astype(bf16)

    def put(self, part, ball, h, value):
        start = part * D + h * HEAD_DIM
        self.d_qkv_t[ball, start : start + HEAD_DIM, :] = value.astype(bf16)

    def value(self, i):
        ball, h = divmod(i, HEADS)
        self.put(2, ball, h, dot(self.d_att[ball][rows_of(h)], self.e_ref[ball, h], 1, 1))

    def query_key(self, i):
        ball, h = divmod(i, HEADS)
        q_t, k_t, _ = self.parts[ball]
        self.put(0, ball, h, dot(k_t[rows_of(h)], self.d_s[ball, h]) * SCALE)
        self.put(1, ball, h, dot(q_t[rows_of(h)], self.d_s[ball, h], 1, 1) * LN2)

    def finish(self, ball):
        values, inv_rms, normed = self.rows.pop(ball)
        d_out, d_qkv_t = self.d_out.pop(ball), self.d_qkv_t[ball]
        self.sums[: 3 * D, :] += dot(d_qkv_t, normed)
        self.sums[3 * D : 4 * D, :] += dot(self.att_ref[ball], d_out)
        d_normed = dot(self.w_ref[...], d_qkv_t).T
        unit = values * inv_rms
        self.sums[4 * D : 4 * D + 1, :] += jnp.sum(d_normed * unit, axis=0, keepdims=True)
        d_unit = d_normed * self.gain_ref[...]
        along = jnp.mean(d_unit * unit, axis=-1, keepdims=True)
        return d_out.astype(f32) + inv_rms * (d_unit - unit * along)


def normalise(values, gain_ref):
    inv_rms = inverse_rms(values)
    return inv_rms, (values * inv_rms * gain_ref[...]).astype(bf16)


def gather(rows, order_ref, from_ref, to_ref):
    for r in rows:
        to_ref[pl.ds(r, 1), :] = from_ref[pl.ds(order_ref[r], 1), :]


def scatter(rows, order_ref, from_ref, to_ref):
    for r in rows:
        to_ref[pl.ds(order_ref[r], 1), :] = from_ref[pl.ds(r, 1), :]


def chunk(i):
    return range(i * CHUNK, (i + 1) * CHUNK)


def arranged(sums):
    gain = sums[4 * D : 4 * D + 16, :]
    parts = [sums[0:D, :].T, sums[D : 2 * D, :].T, gain, sums[2 * D : 3 * D, :].T, sums[3 * D : 4 * D, :], gain]
    return jnp.concatenate(parts, axis=0)


def first_kernel(order_ref, x_ref, gain_ref, w_ref, proj_ref, sent_ref, inverse_ref, inv_ref, e_out, kept_out, v_out, wt, out, sent, e_s, kept, v_s, att_s, sems):
    balls = e_s.shape[0]
    heads = balls * HEADS
    wt[...] = w_ref[...].T
    forward = Forward(e_s, inv_ref, att_s)
    values, copies = {}, []

    def invert(i):
        for r in chunk(i):
            inverse_ref[order_ref[r]] = r

    def prepare(ball):
        values[ball] = x_ref[ball_rows(ball), :].astype(f32)
        _, normed = normalise(values[ball], gain_ref)
        parts = project(normed, w_ref, wt)
        forward.parts[ball] = parts
        kept[ball, D : 2 * D, :] = parts[0]
        kept[ball, 2 * D :, :] = parts[1]
        v_s[ball] = parts[4]

    def finish(ball):
        att_t = att_s[ball]
        kept[ball, :D, :] = att_t
        out[ball_rows(ball), :] = values.pop(ball) + dot(att_t, proj_ref[...], 0, 0)
        for n, (source, target) in enumerate(((e_s, e_out), (kept, kept_out), (v_s, v_out))):
            copy = pltpu.make_async_copy(source.at[ball], target.at[ball], sems.at[n, ball])
            copy.start()
            copies.append(copy)

    early = 2 * HEADS

    def invert_early(i):
        if i < early:
            for n in range(i * heads // early, (i + 1) * heads // early):
                invert(n)

    staggered(
        heads,
        (0, at_first(prepare)),
        (0, invert_early),
        (2, forward.score),
        (6, forward.soften),
        (8, forward.attend),
        (8, at_last(finish)),
        (17, lambda i: scatter(chunk(i), inverse_ref, out, sent)),
    )
    sent_ref[...] = sent[...].astype(bf16)
    for copy in copies:
        copy.wait()


def second_kernel(order_ref, came_ref, d_out_ref, gain_ref, w_ref, proj_ref, sent_ref, grads_ref, wt, came, placed, e_s, inv_s, att_s, d_s, d_qkv_t, d_in, d_came, sums):
    balls = e_s.shape[0]
    wt[...] = w_ref[...].T
    came[...] = came_ref[...].astype(f32)
    sums[...] = jnp.zeros_like(sums)
    forward = Forward(e_s, inv_s, att_s)
    backward = Backward(e_s, inv_s, att_s, d_s, d_qkv_t, w_ref, proj_ref, gain_ref, sums)

    def prepare(ball):
        values = placed[ball_rows(ball), :]
        inv_rms, normed = normalise(values, gain_ref)
        parts = project(normed, w_ref, wt)
        forward.parts[ball] = parts
        backward.parts[ball] = (parts[0], parts[1], parts[4])
        backward.rows[ball] = (values, inv_rms, normed)

    def join(ball):
        backward.join(ball, d_out_ref[ball_rows(ball), :])

    def finish(ball):
        d_in[ball_rows(ball), :] = backward.finish(ball)

    staggered(
        balls * HEADS,
        (0, lambda i: gather(chunk(i), order_ref, came, placed)),
        (8, at_first(prepare)),
        (10, forward.score),
        (14, forward.soften),
        (16, forward.attend),
        (16, at_last(join)),
        (25, backward.weigh),
        (28, backward.score),
        (28, backward.value),
        (30, backward.query_key),
        (30, at_last(finish)),
        (39, lambda i: scatter(chunk(i), order_ref, d_in, d_came)),
    )
    sent_ref[...] = d_came[...].astype(bf16)
    grads_ref[...] = arranged(sums)


def third_kernel(core_ref, inverse_ref, came_ref, x_ref, gain_ref, w_ref, proj_ref, inv_ref, other_ref, e_in, kept_in, v_in, d_x_ref, mine_ref, sent_ref, came, d_first, e_s, kept, v_s, d_s, d_qkv_t, sums, halves, sems):
    balls = e_s.shape[0]
    copies = {}
    for ball in range(balls):
        for n, (source, target) in enumerate(((e_in, e_s), (kept_in, kept), (v_in, v_s))):
            copies[ball, n] = pltpu.make_async_copy(source.at[ball], target.at[ball], sems.at[n, ball])
            copies[ball, n].start()
    came[...] = came_ref[...].astype(f32)
    sums[...] = jnp.zeros_like(sums)
    backward = Backward(e_s, inv_ref, kept.at[:, :D, :], d_s, d_qkv_t, w_ref, proj_ref, gain_ref, sums)

    def prepare(ball):
        for n in range(3):
            copies[ball, n].wait()
        values = x_ref[ball_rows(ball), :].astype(f32)
        inv_rms, normed = normalise(values, gain_ref)
        backward.rows[ball] = (values, inv_rms, normed)
        backward.parts[ball] = (kept[ball, D : 2 * D, :], kept[ball, 2 * D :, :], v_s[ball])
        backward.join(ball, d_first[ball_rows(ball), :].astype(bf16))

    def finish(ball):
        d_x_ref[ball_rows(ball), :] = backward.finish(ball).astype(bf16)

    staggered(
        balls * HEADS,
        (0, lambda i: gather(chunk(i), inverse_ref, came, d_first)),
        (8, at_first(prepare)),
        (10, backward.weigh),
        (13, backward.score),
        (13, backward.value),
        (15, backward.query_key),
        (15, at_last(finish)),
    )
    halves[...] = arranged(sums)
    core = core_ref[0]
    for n, ref in enumerate((halves, other_ref)):
        block = slice(n * GRAD_HALF, (n + 1) * GRAD_HALF)
        mine_ref[block, :] = ref[pl.ds(pl.multiple_of(core * GRAD_HALF, 16), GRAD_HALF), :]
        sent_ref[block, :] = ref[pl.ds(pl.multiple_of((1 - core) * GRAD_HALF, 16), GRAD_HALF), :].astype(bf16)


def last_kernel(core_ref, mine_ref, came_ref, *out_refs):
    first = core_ref[0] == 0
    mine, came = mine_ref[...].astype(f32), came_ref[...].astype(f32)
    low = jnp.where(first, mine, came)
    high = jnp.where(first, came, mine)
    for n in range(2):
        gain_ref, qkv_ref, proj_ref = out_refs[3 * n : 3 * n + 3]
        start = n * GRAD_HALF
        qkv_ref[:, :D] = low[start : start + D]
        qkv_ref[:, D : 2 * D] = low[start + D : start + 2 * D]
        gain_ref[...] = low[start + 2 * D : start + 2 * D + 1]
        qkv_ref[:, 2 * D :] = high[start : start + D]
        proj_ref[...] = high[start + D : start + 2 * D]


SCALARS = pl.BlockSpec(memory_space=pltpu.SMEM)
VECTORS = pl.BlockSpec(memory_space=pltpu.VMEM)
REMAIN = pl.BlockSpec(memory_space=pl.ANY)


def call(kernel, in_specs, outs, scratch):
    return pl.pallas_call(
        kernel,
        in_specs=in_specs,
        out_specs=[spec for spec, _, _ in outs],
        out_shape=[jax.ShapeDtypeStruct(shape, kind) for _, shape, kind in outs],
        scratch_shapes=scratch,
        compiler_params=pltpu.CompilerParams(vmem_limit_bytes=VMEM_LIMIT),
    )


def first_call(order, x, gain, w, proj):
    rows = x.shape[0]
    balls = rows // BALL
    kept = [((balls, HEADS, BALL, BALL), bf16), ((balls, 3 * D, BALL), bf16), ((balls, BALL, D), bf16)]
    return call(
        first_kernel,
        [SCALARS] + [VECTORS] * 4,
        [(VECTORS, (rows, D), bf16), (SCALARS, (rows,), jnp.int32), (VECTORS, (balls, HEADS, BALL), f32)]
        + [(REMAIN, shape, kind) for shape, kind in kept],
        [pltpu.VMEM((3 * D, D), bf16), pltpu.VMEM((rows, D), f32), pltpu.VMEM((rows, D), f32)]
        + [pltpu.VMEM(shape, kind) for shape, kind in kept]
        + [pltpu.VMEM((balls, D, BALL), bf16), pltpu.SemaphoreType.DMA((3, balls))],
    )(order, x, gain, w, proj)


def second_call(order, came, d_out, gain, w, proj):
    rows = came.shape[0]
    balls = rows // BALL
    weights = pltpu.VMEM((balls, HEADS, BALL, BALL), bf16)
    return call(
        second_kernel,
        [SCALARS] + [VECTORS] * 5,
        [(VECTORS, (rows, D), bf16), (VECTORS, (2 * GRAD_HALF, D), f32)],
        [
            pltpu.VMEM((3 * D, D), bf16),
            pltpu.VMEM((rows, D), f32),
            pltpu.VMEM((rows, D), f32),
            weights,
            pltpu.VMEM((balls, HEADS, BALL), f32),
            pltpu.VMEM((balls, D, BALL), bf16),
            weights,
            pltpu.VMEM((balls, 3 * D, BALL), bf16),
            pltpu.VMEM((rows, D), f32),
            pltpu.VMEM((rows, D), f32),
            pltpu.VMEM((4 * D + 16, D), f32),
        ],
    )(order, came, d_out, gain, w, proj)


def third_call(core, inverse, came, x, gain, w, proj, inv, other, kept):
    rows = came.shape[0]
    balls = rows // BALL
    weights = pltpu.VMEM((balls, HEADS, BALL, BALL), bf16)
    return call(
        third_kernel,
        [SCALARS] * 2 + [VECTORS] * 7 + [REMAIN] * 3,
        [(VECTORS, (rows, D), bf16), (VECTORS, (2 * GRAD_HALF, D), f32), (VECTORS, (2 * GRAD_HALF, D), bf16)],
        [pltpu.VMEM((rows, D), f32), pltpu.VMEM((rows, D), f32)]
        + [pltpu.VMEM(part.shape, part.dtype) for part in kept]
        + [
            weights,
            pltpu.VMEM((balls, 3 * D, BALL), bf16),
            pltpu.VMEM((4 * D + 16, D), f32),
            pltpu.VMEM((2 * GRAD_HALF, D), f32),
            pltpu.SemaphoreType.DMA((3, balls)),
        ],
    )(core, inverse, came, x, gain, w, proj, inv, other, *kept)


def last_call(core, mine, came):
    shapes = [(1, D), (D, 3 * D), (D, D)] * 2
    return call(last_kernel, [SCALARS] + [VECTORS] * 2, [(VECTORS, shape, f32) for shape in shapes], [])(core, mine, came)


def exchange(rows):
    return lax.all_to_all(rows, "wide", split_axis=0, concat_axis=0, tiled=True)


def swap(part, peers, apart):
    return lax.ppermute(part, "wide", [(i, i ^ apart) for i in range(peers)])


def body(tokens, cotangent, order_send, order_recv, gain_a, qkv_a, proj_a, gain_b, qkv_b, proj_b):
    peers = lax.axis_size("wide")
    core = (lax.axis_index("wide") % 2).astype(jnp.int32).reshape(1)
    gain_a = gain_a.reshape(1, D)
    gain_b = gain_b.reshape(1, D)
    sent, inverse, inv, *kept = first_call(order_send, tokens, gain_a, qkv_a, proj_a)
    d_sent, grads_b = second_call(order_recv, exchange(sent), cotangent, gain_b, qkv_b, proj_b)
    d_tokens, mine, other = third_call(
        core, inverse, exchange(d_sent), tokens, gain_a, qkv_a, proj_a, inv, grads_b, kept
    )
    total = mine + swap(other, peers, 1).astype(f32)
    apart = 2
    while apart < peers:
        part = total.astype(bf16)
        total = part.astype(f32) + swap(part, peers, apart).astype(f32)
        apart *= 2
    part = total.astype(bf16)
    sums = last_call(core, part, swap(part, peers, 1))
    d_gain_a, d_qkv_a, d_proj_a, d_gain_b, d_qkv_b, d_proj_b = sums
    return d_tokens, d_gain_a.reshape(D), d_qkv_a, d_proj_a, d_gain_b.reshape(D), d_qkv_b, d_proj_b


def solution(mesh):
    rows = P(("grp", "wide"), None)
    order = P(("grp", "wide"))
    return jax.shard_map(
        body,
        mesh=mesh,
        in_specs=(rows, rows, order, order) + (P(),) * 6,
        out_specs=(rows,) + (P("grp"), P("grp", None), P("grp", None)) * 2,
        check_vma=False,
    )
```

time: 337 us -> 110 us (0.33); the launches traced: 331 us -> 110 us
  matrix products: 102 us -> 0 us
  waiting for transfers between devices: 105 us -> 31.2 us
  Pallas kernels: 0 us -> 44.1 us
  local copies, waits for them, and re-layouts: 41 us -> 1.46 us
  other arithmetic: 23.8 us -> 1.11 us
  between operations: 15.1 us -> 0.71 us
  blocking collectives: 32.6 us -> 22 us
    psum x1 -> x0, waiting for transfers between devices: 86.6 us -> none  [body(): lax.psum((d_gain_a, d_qkv_a, d_proj_a, d_gain_b, d_qkv_b, d_proj_b), 'wide')]
    dot_general x21 -> x0, matrix products: 84.1 us -> none  [the longest x4 39.6 us: ball_core(): jnp.einsum('bqhd,bkhd->bhqk', query, keys, preferred_element_type=jnp.flo...]
    pallas_call x0 -> x4, Pallas kernels: none -> 44.1 us  [the longest x1 17.4 us: second_call(): call(second_kernel, [SCALARS] + [VECTORS] * 5, [(VECTORS, (rows, D), bf16...]
    psum x1 -> x0, blocking collectives: 32.6 us -> none  [body(): lax.psum((d_gain_a, d_qkv_a, d_proj_a, d_gain_b, d_qkv_b, d_proj_b), 'wide')]
    all_to_all x0 -> x1, blocking collectives: none -> 22 us  [exchange(): return lax.all_to_all(rows, 'wide', split_axis=0, concat_axis=0, tiled=True)]
    sub x2 -> x0, matrix products: 17.9 us -> none  [ball_core(): weights = jax.nn.softmax(scores, axis=-1).astype(jnp.bfloat16)]
    ppermute x0 -> x5, waiting for transfers between devices: none -> 16.7 us  [swap(): return lax.ppermute(part, 'wide', [(i, i ^ apart) for i in range(peers)])]
    unnamed x72 -> x6, local copies, waits for them, and re-layouts: 15.8 us -> 1.46 us
  transfers between devices with their start and end apart: 3 -> 6, of which waited for: 3 -> 6; matrix products, arithmetic and copies ran while one was open for 4% -> 0% of each run, Pallas kernels for 0% -> 0%
where the time goes in v2:
time: 110 us
  Pallas kernels  44.1 us (40%)
  waiting for transfers between devices  31.2 us (28%)
  blocking collectives  22 us (20%)
  starting transfers between devices  9.15 us (8%)
  local copies, waits for them, and re-layouts  1.46 us (1%)
  other arithmetic  1.11 us (1%)
    all_to_all x1, blocking collectives, exchange(): return lax.all_to_all(rows, 'wide', split_axis=0, concat_axis=0, tiled=True)  22 us
    pallas_call x1, Pallas kernels, second_call(): call(second_kernel, [SCALARS] + [VECTORS] * 5, [(VECTORS, (rows, D), bf16...  17.4 us
    ppermute x5, waiting for transfers between devices, swap(): return lax.ppermute(part, 'wide', [(i, i ^ apart) for i in range(peers)])  16.7 us
    all_to_all x1, waiting for transfers between devices, exchange(): return lax.all_to_all(rows, 'wide', split_axis=0, concat_axis=0, tiled=True)  14.5 us
    pallas_call x1, Pallas kernels, third_call(): call(third_kernel, [SCALARS] * 2 + [VECTORS] * 7 + [REMAIN] * 3, [(VECTOR...  13.9 us
    pallas_call x1, Pallas kernels, first_call(): call(first_kernel, [SCALARS] + [VECTORS] * 4, [(VECTORS, (rows, D), bf16)...  10.9 us
    ppermute x5, starting transfers between devices, swap(): return lax.ppermute(part, 'wide', [(i, i ^ apart) for i in range(peers)])  5.05 us
    all_to_all x1, starting transfers between devices, exchange(): return lax.all_to_all(rows, 'wide', split_axis=0, concat_axis=0, tiled=True)  4.1 us
  transfers between devices with their start and end apart: 6, of which 6 were waited for; matrix products, arithmetic and copies ran while one was open for 0% of the time, Pallas kernels for 0%

profile of v2, /device:TPU:0, one launch (start us, length us, event | category | flops | bytes accessed | tf_op | source)
XLA Modules:
  0.0 109.7 jit_solution(5381454656550425197)
XLA Ops:
  0.6 10.9 %shard_map.153 = (bf16[2048,128]{1,0:T(8,128)(2,1)}, s32[2048]{0:T(1024)}, f32[8,8,256]{2,1,0:T(8,128)}, bf16[8,8,256,256]{3,2,1,0:T(8,128)(2,1)}, bf16[8,384,25...) custom-call(s32[2048]{0:T(1024)} %order_ref.2, bf16[2048,128]{1,0:T(8,128)(2,1)} %x_ref.3, f32[1,128]{1,0:T(1,128)} %bitcast.13, ...), custom_call_target="tpu_custom_call" | custom-call | tf_op jit(solution)/shard_map/pallas_call | solution.py:337
  11.6 22.0 %all_to_all.22 = bf16[16,128,128]{2,1,0:T(8,128)(2,1)} all-to-all(bf16[16,128,128]{2,1,0:T(8,128)(2,1)} %bitcast.12), channel_id=1, replica_groups=mesh['wide'=16,'grp'=2] {'wide'}, dimensions={0} | all-to-all | bytes 1048576 | tf_op jit(solution)/shard_map/all_to_all | solution.py:398
  33.5 17.4 %shard_map.154 = (bf16[2048,128]{1,0:T(8,128)(2,1)}, f32[544,128]{1,0:T(8,128)}) custom-call(s32[2048]{0:T(1024)} %order_ref.3, bf16[2048,128]{1,0:T(8,128)(2,1)} %bitcast.9, bf16[2048,128]{1,0:T(8,128)(2,1)} %d_out_ref.1, f32[1,128]{1,0:T(1,128)} %bitcast.15, bf16[128,384]{1,0:T(8,128)(2,1)} %w_ref.4, bf16[128,128]{1,0:T(8,128)(2,1)} %proj_ref.4), custom_call_target="tpu_custom_call" | custom-call | tf_op jit(solution)/shard_map/pallas_call | solution.py:352
  51.0 4.1 %all-to-all-start.1 = ((bf16[16,128,128]{2,1,0:T(8,128)(2,1)}), bf16[16,128,128]{2,1,0:T(8,128)(2,1)S(1)}, u32[]{:S(2)}, u32[]{:S(2)}) async-start(bf16[16,128,128]{2,1,0:T(8,128)(2,1)} %bitcast.11), calls=%async_computation.1 | async-start | bytes 1048576 | tf_op jit(solution)/shard_map/all_to_all | solution.py:398
  55.1 14.5 %all-to-all-done.1 = bf16[16,128,128]{2,1,0:T(8,128)(2,1)S(1)} async-done(((bf16[16,128,128]{2,1,0:T(8,128)(2,1)}), bf16[16,128,128]{2,1,0:T(8,128)(2,1)S(1)}, u32[]{:S(2)}, u32[]{:S(2)}) %all-to-all-start.1) | async-done | bytes 524320 | tf_op jit(solution)/shard_map/all_to_all | solution.py:398
  69.6 0.0 copy-start
  69.6 0.8 copy-done
  70.4 13.9 %shard_map.155 = (bf16[2048,128]{1,0:T(8,128)(2,1)}, f32[544,128]{1,0:T(8,128)}, bf16[544,128]{1,0:T(8,128)(2,1)}) custom-call(s32[1]{0:T(128)} %bitcast.core_ref, s32[2048]{0:T(1024)} %get-tuple-element.24.inverse_ref, bf16[2048,128]{1,0:T(8,128)(2,1)} %bitcast.10, bf16[2048,128]{1,0:T(8,128)(2,1)} %x_ref.3, f32[1,128]{1,0:T(1,128)} %bitcast.14, ...), custom_call_target="tpu_custom_call" | custom-call | tf_op jit(solution)/shard_map/pallas_call | solution.py:376
  84.3 0.1 collective-permute-start
  84.4 1.5 %collective-permute-done = bf16[544,128]{1,0:T(8,128)(2,1)S(1)} collective-permute-done((bf16[544,128]{1,0:T(8,128)(2,1)}, bf16[544,128]{1,0:T(8,128)(2,1)S(1)}, u32[]{:S(2)}, u32[]{:S(2)}) %collective-permute-start) | collective-permute-done | bytes 139296 | tf_op jit(solution)/shard_map/ppermute | solution.py:402
  86.0 1.0 add_convert_fusion.3
  87.0 0.9 collective-permute-start.1
  87.8 4.9 %collective-permute-done.1 = bf16[544,128]{1,0:T(8,128)(2,1)S(1)} collective-permute-done((bf16[544,128]{1,0:T(8,128)(2,1)S(1)}, bf16[544,128]{1,0:T(8,128)(2,1)S(1)}, u32[]{:S(2)}, u32[]{:S(2)}) %collective-permute-start.1) | collective-permute-done | bytes 139296 | tf_op jit(solution)/shard_map/ppermute | solution.py:402
  92.8 1.7 %collective-permute-start.2 = (bf16[544,128]{1,0:T(8,128)(2,1)S(1)}, bf16[544,128]{1,0:T(8,128)(2,1)S(1)}, u32[]{:S(2)}, u32[]{:S(2)}) collective-permute-start(bf16[544,128]{1,0:T(8,128)(2,1)S(1)} %add_convert_fusion.2), channel_id=1, source_target_pairs={{0,8},{2,10},{4,12},{6,14},{8,0},{10,2},{12,4},{14,6},{16,24},{18,... | collective-permute-start | bytes 417800 | tf_op jit(solution)/shard_map/ppermute | solution.py:402
  94.5 3.4 %collective-permute-done.2 = bf16[544,128]{1,0:T(8,128)(2,1)S(1)} collective-permute-done((bf16[544,128]{1,0:T(8,128)(2,1)S(1)}, bf16[544,128]{1,0:T(8,128)(2,1)S(1)}, u32[]{:S(2)}, u32[]{:S(2)}) %collective-permute-start.2) | collective-permute-done | bytes 139296 | tf_op jit(solution)/shard_map/ppermute | solution.py:402
  98.0 2.3 %collective-permute-start.3 = (bf16[544,128]{1,0:T(8,128)(2,1)S(1)}, bf16[544,128]{1,0:T(8,128)(2,1)S(1)}, u32[]{:S(2)}, u32[]{:S(2)}) collective-permute-start(bf16[544,128]{1,0:T(8,128)(2,1)S(1)} %add_convert_fusion.1), channel_id=1, source_target_pairs={{0,16},{2,18},{4,20},{6,22},{8,24},{10,26},{12,28},{14,30},{16,0},... | collective-permute-start | bytes 417800 | tf_op jit(solution)/shard_map/ppermute | solution.py:402
  100.3 5.5 %collective-permute-done.3 = bf16[544,128]{1,0:T(8,128)(2,1)S(1)} collective-permute-done((bf16[544,128]{1,0:T(8,128)(2,1)S(1)}, bf16[544,128]{1,0:T(8,128)(2,1)S(1)}, u32[]{:S(2)}, u32[]{:S(2)}) %collective-permute-start.3) | collective-permute-done | bytes 139296 | tf_op jit(solution)/shard_map/ppermute | solution.py:402
  105.8 0.0 copy-start.1
  105.8 0.1 collective-permute-start.4
  105.9 1.3 %collective-permute-done.4.came_ref = bf16[544,128]{1,0:T(8,128)(2,1)S(1)} collective-permute-done((bf16[544,128]{1,0:T(8,128)(2,1)S(1)}, bf16[544,128]{1,0:T(8,128)(2,1)S(1)}, u32[]{:S(2)}, u32[]{:S(2)}) %collective-permute-start.4) | collective-permute-done | bytes 139296 | tf_op jit(solution)/shard_map/ppermute | solution.py:402
  107.2 0.0 copy-done.1
  107.2 0.0 copy-start.2
  107.2 0.6 copy-done.2
  107.9 1.8 %shard_map.156 = (f32[1,128]{1,0:T(1,128)}, f32[128,384]{1,0:T(8,128)}, f32[128,128]{1,0:T(8,128)}, f32[1,128]{1,0:T(1,128)}, f32[128,384]{1,0:T(8,128)}, /*index=5*/f32[128,128]{1,0:T(8,128)}) custom-call(s32[1]{0:T(128)} %bitcast.core_ref, bf16[544,128]{1,0:T(8,128)(2,1)} %copy-done.1, bf16[544,128]{1,0:T(8,128)(2,1)} %copy-done.2), custom_call_target="tpu_custom_call" | custom-call | tf_op jit(solution)/shard_map/pallas_call | solution.py:394
  (3 shorter events, 0.1 us)
Async XLA Ops:
  51.0 18.6 %all-to-all-start.1 = ((bf16[16,128,128]{2,1,0:T(8,128)(2,1)}), bf16[16,128,128]{2,1,0:T(8,128)(2,1)S(1)}, u32[]{:S(2)}, u32[]{:S(2)}) async-start(bf16[16,128,128]{2,1,0:T(8,128)(2,1)} %bitcast.11), calls=%async_computation.1 | async-start | bytes 1048576 | tf_op jit(solution)/shard_map/all_to_all | solution.py:398
  69.6 0.8 copy-start
  84.3 1.6 %collective-permute-start = (bf16[544,128]{1,0:T(8,128)(2,1)}, bf16[544,128]{1,0:T(8,128)(2,1)S(1)}, u32[]{:S(2)}, u32[]{:S(2)}) collective-permute-start(bf16[544,128]{1,0:T(8,128)(2,1)} %get-tuple-element.34), channel_id=1, source_target_pairs={{0,2},{2,0},{4,6},{6,4},{8,10},{10,8},{12,14},{14,12},{16,18},{18,... | collective-permute-start | bytes 417800 | tf_op jit(solution)/shard_map/ppermute | solution.py:402
  87.0 5.8 %collective-permute-start.1 = (bf16[544,128]{1,0:T(8,128)(2,1)S(1)}, bf16[544,128]{1,0:T(8,128)(2,1)S(1)}, u32[]{:S(2)}, u32[]{:S(2)}) collective-permute-start(bf16[544,128]{1,0:T(8,128)(2,1)S(1)} %add_convert_fusion.3), channel_id=1, source_target_pairs={{0,4},{2,6},{4,0},{6,2},{8,12},{10,14},{12,8},{14,10},{16,20},{18,... | collective-permute-start | bytes 417800 | tf_op jit(solution)/shard_map/ppermute | solution.py:402
  92.8 5.1 %collective-permute-start.2 = (bf16[544,128]{1,0:T(8,128)(2,1)S(1)}, bf16[544,128]{1,0:T(8,128)(2,1)S(1)}, u32[]{:S(2)}, u32[]{:S(2)}) collective-permute-start(bf16[544,128]{1,0:T(8,128)(2,1)S(1)} %add_convert_fusion.2), channel_id=1, source_target_pairs={{0,8},{2,10},{4,12},{6,14},{8,0},{10,2},{12,4},{14,6},{16,24},{18,... | collective-permute-start | bytes 417800 | tf_op jit(solution)/shard_map/ppermute | solution.py:402
  98.0 7.8 %collective-permute-start.3 = (bf16[544,128]{1,0:T(8,128)(2,1)S(1)}, bf16[544,128]{1,0:T(8,128)(2,1)S(1)}, u32[]{:S(2)}, u32[]{:S(2)}) collective-permute-start(bf16[544,128]{1,0:T(8,128)(2,1)S(1)} %add_convert_fusion.1), channel_id=1, source_target_pairs={{0,16},{2,18},{4,20},{6,22},{8,24},{10,26},{12,28},{14,30},{16,0},... | collective-permute-start | bytes 417800 | tf_op jit(solution)/shard_map/ppermute | solution.py:402
  105.8 1.4 %copy-start.1 = (bf16[544,128]{1,0:T(8,128)(2,1)}, bf16[544,128]{1,0:T(8,128)(2,1)S(1)}, u32[]{:S(2)}) copy-start(bf16[544,128]{1,0:T(8,128)(2,1)S(1)} %add_convert_fusion.mine_ref) | copy-start | bytes 417796
  105.8 1.4 %collective-permute-start.4 = (bf16[544,128]{1,0:T(8,128)(2,1)S(1)}, bf16[544,128]{1,0:T(8,128)(2,1)S(1)}, u32[]{:S(2)}, u32[]{:S(2)}) collective-permute-start(bf16[544,128]{1,0:T(8,128)(2,1)S(1)} %add_convert_fusion.mine_ref), channel_id=1, source_target_pairs={{0,2},{2,0},{4,6},{6,4},{8,10},{10,8},{12,14},{14,12},{16,18},{18,... | collective-permute-start | bytes 417800 | tf_op jit(solution)/shard_map/ppermute | solution.py:402
  107.2 0.7 copy-start.2

commit v3 on v2

--- a/solution.py
+++ b/solution.py
@@ -14,6 +14,8 @@
 LN2 = 0.6931471805599453
 SCALE = HEAD_DIM ** (-0.5)
 VMEM_LIMIT = 56 * 1024 * 1024
+UNROLL = 32
+AHEAD = 3
 CHUNK = BALL // HEADS
 GRAD_HALF = 2 * D + 16
 
@@ -146,18 +148,37 @@
     return inv_rms, (values * inv_rms * gain_ref[...]).astype(bf16)
 
 
-def gather(rows, order_ref, from_ref, to_ref):
-    for r in rows:
+def for_rows(count, copy_row):
+    def step(i, carry):
+        for j in range(UNROLL):
+            copy_row(i * UNROLL + j)
+        return carry
+
+    lax.fori_loop(0, count // UNROLL, step, 0)
+
+
+def gather_chunk(i, order_ref, from_ref, to_ref):
+    for r in range(i * CHUNK, (i + 1) * CHUNK):
         to_ref[pl.ds(r, 1), :] = from_ref[pl.ds(order_ref[r], 1), :]
 
 
-def scatter(rows, order_ref, from_ref, to_ref):
-    for r in rows:
+def scatter_chunk(i, order_ref, from_ref, to_ref):
+    for r in range(i * CHUNK, (i + 1) * CHUNK):
         to_ref[pl.ds(order_ref[r], 1), :] = from_ref[pl.ds(r, 1), :]
 
 
-def chunk(i):
-    return range(i * CHUNK, (i + 1) * CHUNK)
+def gather(order_ref, from_ref, to_ref):
+    def copy_row(r):
+        to_ref[pl.ds(r, 1), :] = from_ref[pl.ds(order_ref[r], 1), :]
+
+    for_rows(to_ref.shape[0], copy_row)
+
+
+def scatter(order_ref, from_ref, to_ref):
+    def copy_row(r):
+        to_ref[pl.ds(order_ref[r], 1), :] = from_ref[pl.ds(r, 1), :]
+
+    for_rows(from_ref.shape[0], copy_row)
 
 
 def arranged(sums):
@@ -166,16 +187,19 @@
     return jnp.concatenate(parts, axis=0)
 
 
-def first_kernel(order_ref, x_ref, gain_ref, w_ref, proj_ref, sent_ref, inverse_ref, inv_ref, e_out, kept_out, v_out, wt, out, sent, e_s, kept, v_s, att_s, sems):
+def share(core_ref, sums, halves, mine_ref, other_ref):
+    halves[...] = arranged(sums)
+    core = core_ref[0]
+    mine_ref[...] = halves[pl.ds(pl.multiple_of(core * GRAD_HALF, 16), GRAD_HALF), :]
+    other_ref[...] = halves[pl.ds(pl.multiple_of((1 - core) * GRAD_HALF, 16), GRAD_HALF), :].astype(bf16)
+
+
+def first_kernel(order_ref, x_ref, gain_ref, w_ref, proj_ref, sent_ref, inv_ref, e_out, kept_out, v_out, wt, out, sent, e_s, kept, v_s, att_s, sems):
     balls = e_s.shape[0]
     heads = balls * HEADS
     wt[...] = w_ref[...].T
     forward = Forward(e_s, inv_ref, att_s)
     values, copies = {}, []
-
-    def invert(i):
-        for r in chunk(i):
-            inverse_ref[order_ref[r]] = r
 
     def prepare(ball):
         values[ball] = x_ref[ball_rows(ball), :].astype(f32)
@@ -195,29 +219,21 @@
             copy.start()
             copies.append(copy)
 
-    early = 2 * HEADS
-
-    def invert_early(i):
-        if i < early:
-            for n in range(i * heads // early, (i + 1) * heads // early):
-                invert(n)
-
     staggered(
         heads,
         (0, at_first(prepare)),
-        (0, invert_early),
         (2, forward.score),
         (6, forward.soften),
         (8, forward.attend),
         (8, at_last(finish)),
-        (17, lambda i: scatter(chunk(i), inverse_ref, out, sent)),
     )
+    gather(order_ref, out, sent)
     sent_ref[...] = sent[...].astype(bf16)
     for copy in copies:
         copy.wait()
 
 
-def second_kernel(order_ref, came_ref, d_out_ref, gain_ref, w_ref, proj_ref, sent_ref, grads_ref, wt, came, placed, e_s, inv_s, att_s, d_s, d_qkv_t, d_in, d_came, sums):
+def second_kernel(core_ref, order_ref, came_ref, d_out_ref, gain_ref, w_ref, proj_ref, sent_ref, mine_ref, other_ref, wt, came, placed, e_s, inv_s, att_s, d_s, d_qkv_t, d_in, d_came, sums, halves):
     balls = e_s.shape[0]
     wt[...] = w_ref[...].T
     came[...] = came_ref[...].astype(f32)
@@ -241,7 +257,7 @@
 
     staggered(
         balls * HEADS,
-        (0, lambda i: gather(chunk(i), order_ref, came, placed)),
+        (0, lambda i: gather_chunk(i, order_ref, came, placed)),
         (8, at_first(prepare)),
         (10, forward.score),
         (14, forward.soften),
@@ -252,26 +268,30 @@
         (28, backward.value),
         (30, backward.query_key),
         (30, at_last(finish)),
-        (39, lambda i: scatter(chunk(i), order_ref, d_in, d_came)),
+        (39, lambda i: scatter_chunk(i, order_ref, d_in, d_came)),
     )
     sent_ref[...] = d_came[...].astype(bf16)
-    grads_ref[...] = arranged(sums)
-
-
-def third_kernel(core_ref, inverse_ref, came_ref, x_ref, gain_ref, w_ref, proj_ref, inv_ref, other_ref, e_in, kept_in, v_in, d_x_ref, mine_ref, sent_ref, came, d_first, e_s, kept, v_s, d_s, d_qkv_t, sums, halves, sems):
+    share(core_ref, sums, halves, mine_ref, other_ref)
+
+
+def third_kernel(core_ref, order_ref, came_ref, x_ref, gain_ref, w_ref, proj_ref, inv_ref, e_in, kept_in, v_in, d_x_ref, mine_ref, other_ref, came, d_first, e_s, kept, v_s, d_s, d_qkv_t, sums, halves, sems):
     balls = e_s.shape[0]
     copies = {}
     for ball in range(balls):
         for n, (source, target) in enumerate(((e_in, e_s), (kept_in, kept), (v_in, v_s))):
             copies[ball, n] = pltpu.make_async_copy(source.at[ball], target.at[ball], sems.at[n, ball])
-            copies[ball, n].start()
+            if ball < AHEAD:
+                copies[ball, n].start()
     came[...] = came_ref[...].astype(f32)
     sums[...] = jnp.zeros_like(sums)
+    scatter(order_ref, came, d_first)
     backward = Backward(e_s, inv_ref, kept.at[:, :D, :], d_s, d_qkv_t, w_ref, proj_ref, gain_ref, sums)
 
     def prepare(ball):
         for n in range(3):
             copies[ball, n].wait()
+            if ball + AHEAD < balls:
+                copies[ball + AHEAD, n].start()
         values = x_ref[ball_rows(ball), :].astype(f32)
         inv_rms, normed = normalise(values, gain_ref)
         backward.rows[ball] = (values, inv_rms, normed)
@@ -283,35 +303,34 @@
 
     staggered(
         balls * HEADS,
-        (0, lambda i: gather(chunk(i), inverse_ref, came, d_first)),
-        (8, at_first(prepare)),
-        (10, backward.weigh),
-        (13, backward.score),
-        (13, backward.value),
-        (15, backward.query_key),
-        (15, at_last(finish)),
+        (0, at_first(prepare)),
+        (2, backward.weigh),
+        (5, backward.score),
+        (5, backward.value),
+        (7, backward.query_key),
+        (7, at_last(finish)),
     )
-    halves[...] = arranged(sums)
-    core = core_ref[0]
-    for n, ref in enumerate((halves, other_ref)):
-        block = slice(n * GRAD_HALF, (n + 1) * GRAD_HALF)
-        mine_ref[block, :] = ref[pl.ds(pl.multiple_of(core * GRAD_HALF, 16), GRAD_HALF), :]
-        sent_ref[block, :] = ref[pl.ds(pl.multiple_of((1 - core) * GRAD_HALF, 16), GRAD_HALF), :].astype(bf16)
-
-
-def last_kernel(core_ref, mine_ref, came_ref, *out_refs):
+    share(core_ref, sums, halves, mine_ref, other_ref)
+
+
+def last_kernel(core_ref, mine_a, came_a, mine_b, came_b, *refs):
+    outs, parts, sems = refs[:6], refs[6:10], refs[10]
+    copies = [pltpu.make_async_copy(ref, part, sems.at[n]) for n, (ref, part) in enumerate(zip((mine_a, came_a, mine_b, came_b), parts))]
+    for copy in copies:
+        copy.start()
     first = core_ref[0] == 0
-    mine, came = mine_ref[...].astype(f32), came_ref[...].astype(f32)
-    low = jnp.where(first, mine, came)
-    high = jnp.where(first, came, mine)
     for n in range(2):
-        gain_ref, qkv_ref, proj_ref = out_refs[3 * n : 3 * n + 3]
-        start = n * GRAD_HALF
-        qkv_ref[:, :D] = low[start : start + D]
-        qkv_ref[:, D : 2 * D] = low[start + D : start + 2 * D]
-        gain_ref[...] = low[start + 2 * D : start + 2 * D + 1]
-        qkv_ref[:, 2 * D :] = high[start : start + D]
-        proj_ref[...] = high[start + D : start + 2 * D]
+        gain_ref, qkv_ref, proj_ref = outs[3 * n : 3 * n + 3]
+        copies[2 * n].wait()
+        copies[2 * n + 1].wait()
+        mine, came = parts[2 * n][...].astype(f32), parts[2 * n + 1][...].astype(f32)
+        low = jnp.where(first, mine, came)
+        high = jnp.where(first, came, mine)
+        qkv_ref[:, :D] = low[:D]
+        qkv_ref[:, D : 2 * D] = low[D : 2 * D]
+        gain_ref[...] = low[2 * D : 2 * D + 1]
+        qkv_ref[:, 2 * D :] = high[:D]
+        proj_ref[...] = high[D : 2 * D]
 
 
 SCALARS = pl.BlockSpec(memory_space=pltpu.SMEM)
@@ -337,7 +356,7 @@
     return call(
         first_kernel,
         [SCALARS] + [VECTORS] * 4,
-        [(VECTORS, (rows, D), bf16), (SCALARS, (rows,), jnp.int32), (VECTORS, (balls, HEADS, BALL), f32)]
+        [(VECTORS, (rows, D), bf16), (VECTORS, (balls, HEADS, BALL), f32)]
         + [(REMAIN, shape, kind) for shape, kind in kept],
         [pltpu.VMEM((3 * D, D), bf16), pltpu.VMEM((rows, D), f32), pltpu.VMEM((rows, D), f32)]
         + [pltpu.VMEM(shape, kind) for shape, kind in kept]
@@ -345,14 +364,14 @@
     )(order, x, gain, w, proj)
 
 
-def second_call(order, came, d_out, gain, w, proj):
+def second_call(core, order, came, d_out, gain, w, proj):
     rows = came.shape[0]
     balls = rows // BALL
     weights = pltpu.VMEM((balls, HEADS, BALL, BALL), bf16)
     return call(
         second_kernel,
-        [SCALARS] + [VECTORS] * 5,
-        [(VECTORS, (rows, D), bf16), (VECTORS, (2 * GRAD_HALF, D), f32)],
+        [SCALARS] * 2 + [VECTORS] * 5,
+        [(VECTORS, (rows, D), bf16), (VECTORS, (GRAD_HALF, D), f32), (VECTORS, (GRAD_HALF, D), bf16)],
         [
             pltpu.VMEM((3 * D, D), bf16),
             pltpu.VMEM((rows, D), f32),
@@ -365,18 +384,19 @@
             pltpu.VMEM((rows, D), f32),
             pltpu.VMEM((rows, D), f32),
             pltpu.VMEM((4 * D + 16, D), f32),
+            pltpu.VMEM((2 * GRAD_HALF, D), f32),
         ],
-    )(order, came, d_out, gain, w, proj)
-
-
-def third_call(core, inverse, came, x, gain, w, proj, inv, other, kept):
+    )(core, order, came, d_out, gain, w, proj)
+
+
+def third_call(core, order, came, x, gain, w, proj, inv, kept):
     rows = came.shape[0]
     balls = rows // BALL
     weights = pltpu.VMEM((balls, HEADS, BALL, BALL), bf16)
     return call(
         third_kernel,
-        [SCALARS] * 2 + [VECTORS] * 7 + [REMAIN] * 3,
-        [(VECTORS, (rows, D), bf16), (VECTORS, (2 * GRAD_HALF, D), f32), (VECTORS, (2 * GRAD_HALF, D), bf16)],
+        [SCALARS] * 2 + [VECTORS] * 6 + [REMAIN] * 3,
+        [(VECTORS, (rows, D), bf16), (VECTORS, (GRAD_HALF, D), f32), (VECTORS, (GRAD_HALF, D), bf16)],
         [pltpu.VMEM((rows, D), f32), pltpu.VMEM((rows, D), f32)]
         + [pltpu.VMEM(part.shape, part.dtype) for part in kept]
         + [
@@ -386,12 +406,17 @@
             pltpu.VMEM((2 * GRAD_HALF, D), f32),
             pltpu.SemaphoreType.DMA((3, balls)),
         ],
-    )(core, inverse, came, x, gain, w, proj, inv, other, *kept)
-
-
-def last_call(core, mine, came):
+    )(core, order, came, x, gain, w, proj, inv, *kept)
+
+
+def last_call(core, *parts):
     shapes = [(1, D), (D, 3 * D), (D, D)] * 2
-    return call(last_kernel, [SCALARS] + [VECTORS] * 2, [(VECTORS, shape, f32) for shape in shapes], [])(core, mine, came)
+    return call(
+        last_kernel,
+        [SCALARS] + [REMAIN] * 4,
+        [(VECTORS, shape, f32) for shape in shapes],
+        [pltpu.VMEM((GRAD_HALF, D), bf16)] * 4 + [pltpu.SemaphoreType.DMA((4,))],
+    )(core, *parts)
 
 
 def exchange(rows):
@@ -402,24 +427,39 @@
     return lax.ppermute(part, "wide", [(i, i ^ apart) for i in range(peers)])
 
 
+def sum_cores(mine, other):
+    return mine + swap(other, lax.axis_size("wide"), 1).astype(f32)
+
+
+def sum_chips(total, apart, until):
+    while apart < until:
+        part = total.astype(bf16)
+        total = part.astype(f32) + swap(part, lax.axis_size("wide"), apart).astype(f32)
+        apart *= 2
+    return total
+
+
+def both_halves(total):
+    part = total.astype(bf16)
+    return part, swap(part, lax.axis_size("wide"), 1)
+
+
 def body(tokens, cotangent, order_send, order_recv, gain_a, qkv_a, proj_a, gain_b, qkv_b, proj_b):
-    peers = lax.axis_size("wide")
     core = (lax.axis_index("wide") % 2).astype(jnp.int32).reshape(1)
     gain_a = gain_a.reshape(1, D)
     gain_b = gain_b.reshape(1, D)
-    sent, inverse, inv, *kept = first_call(order_send, tokens, gain_a, qkv_a, proj_a)
-    d_sent, grads_b = second_call(order_recv, exchange(sent), cotangent, gain_b, qkv_b, proj_b)
-    d_tokens, mine, other = third_call(
-        core, inverse, exchange(d_sent), tokens, gain_a, qkv_a, proj_a, inv, grads_b, kept
-    )
-    total = mine + swap(other, peers, 1).astype(f32)
-    apart = 2
-    while apart < peers:
-        part = total.astype(bf16)
-        total = part.astype(f32) + swap(part, peers, apart).astype(f32)
-        apart *= 2
-    part = total.astype(bf16)
-    sums = last_call(core, part, swap(part, peers, 1))
+    sent, inv, *kept = first_call(order_send, tokens, gain_a, qkv_a, proj_a)
+    d_sent, *grads_b = second_call(core, order_recv, exchange(sent), cotangent, gain_b, qkv_b, proj_b)
+    came = exchange(d_sent)
+    peers = lax.axis_size("wide")
+    total_b = sum_chips(sum_cores(*grads_b), 2, peers // 2)
+    came, total_b = lax.optimization_barrier((came, total_b))
+    total_b = sum_chips(total_b, peers // 2, peers)
+    d_tokens, *grads_a = third_call(core, order_send, came, tokens, gain_a, qkv_a, proj_a, inv, kept)
+    grads_a, total_b = lax.optimization_barrier((grads_a, total_b))
+    sums_b = both_halves(total_b)
+    sums_a = both_halves(sum_chips(sum_cores(*grads_a), 2, peers))
+    sums = last_call(core, *sums_a, *sums_b)
     d_gain_a, d_qkv_a, d_proj_a, d_gain_b, d_qkv_b, d_proj_b = sums
     return d_tokens, d_gain_a.reshape(D), d_qkv_a, d_proj_a, d_gain_b.reshape(D), d_qkv_b, d_proj_b
 

time: 110 us -> 107 us (0.973)
  blocking collectives: 22 us -> 0 us
  starting transfers between devices: 9.15 us -> 21.6 us
  waiting for transfers between devices: 31.2 us -> 37 us
    all_to_all x1 -> x0, blocking collectives: 22 us -> none  [exchange(): return lax.all_to_all(rows, 'wide', split_axis=0, concat_axis=0, tiled=True)]
    all_to_all x1 -> x2, starting transfers between devices: 4.1 us -> 11.7 us  [exchange(): return lax.all_to_all(rows, 'wide', split_axis=0, concat_axis=0, tiled=True)]
    ppermute x5 -> x10, starting transfers between devices: 5.05 us -> 9.91 us  [swap(): return lax.ppermute(part, 'wide', [(i, i ^ apart) for i in range(peers)])]
    ppermute x5 -> x10, waiting for transfers between devices: 16.7 us -> 21.5 us  [swap(): return lax.ppermute(part, 'wide', [(i, i ^ apart) for i in range(peers)])]
    all_to_all x1 -> x2, waiting for transfers between devices: 14.5 us -> 15.4 us  [exchange(): return lax.all_to_all(rows, 'wide', split_axis=0, concat_axis=0, tiled=True)]
  transfers between devices with their start and end apart: 6 -> 12, of which waited for: 6 -> 10; matrix products, arithmetic and copies ran while one was open for 0% -> 1% of each run, Pallas kernels for 0% -> 13%
where the time goes in v3:
time: 107 us
  Pallas kernels  43.8 us (41%)
  waiting for transfers between devices  37 us (35%)
  starting transfers between devices  21.6 us (20%)
  other arithmetic  1.99 us (2%)
  local copies, waits for them, and re-layouts  1.42 us (1%)
    ppermute x10, waiting for transfers between devices, swap(): return lax.ppermute(part, 'wide', [(i, i ^ apart) for i in range(peers)])  21.5 us
    pallas_call x1, Pallas kernels, second_call(): call(second_kernel, [SCALARS] * 2 + [VECTORS] * 5, [(VECTORS, (rows, D),...  17.4 us
    all_to_all x2, waiting for transfers between devices, exchange(): return lax.all_to_all(rows, 'wide', split_axis=0, concat_axis=0, tiled=True)  15.4 us
    pallas_call x1, Pallas kernels, third_call(): call(third_kernel, [SCALARS] * 2 + [VECTORS] * 6 + [REMAIN] * 3, [(VECTOR...  14.2 us
    all_to_all x2, starting transfers between devices, exchange(): return lax.all_to_all(rows, 'wide', split_axis=0, concat_axis=0, tiled=True)  11.7 us
    pallas_call x1, Pallas kernels, first_call(): call(first_kernel, [SCALARS] + [VECTORS] * 4, [(VECTORS, (rows, D), bf16)...  10.4 us
    ppermute x10, starting transfers between devices, swap(): return lax.ppermute(part, 'wide', [(i, i ^ apart) for i in range(peers)])  9.91 us
  transfers between devices with their start and end apart: 12, of which 10 were waited for; matrix products, arithmetic and copies ran while one was open for 1% of the time, Pallas kernels for 13%

profile of v3, /device:TPU:0, one launch (start us, length us, event | category | flops | bytes accessed | tf_op | source)
XLA Modules:
  0.0 106.8 jit_solution(10818024394600518569)
XLA Ops:
  0.6 10.4 %shard_map.153 = (bf16[2048,128]{1,0:T(8,128)(2,1)}, f32[8,8,256]{2,1,0:T(8,128)}, bf16[8,8,256,256]{3,2,1,0:T(8,128)(2,1)}, bf16[8,384,256]{2,1,0:T(8,128)(2,1)}, bf16[8,256,128]{2,1,0:T(8,128)(2,1)}) custom-call(s32[2048]{0:T(1024)} %order_ref.5, bf16[2048,128]{1,0:T(8,128)(2,1)} %x_ref.3, f32[1,128]{1,0:T(1,128)} %bitcast.13, bf16[128,384]{1,0:T(8,128)(2,1)} %w_ref.5, ...), custom_call_target="tpu_custom_call" | custom-call | tf_op jit(solution)/shard_map/pallas_call | solution.py:356
  11.0 7.6 %all-to-all-start = ((bf16[16,128,128]{2,1,0:T(8,128)(2,1)}), bf16[16,128,128]{2,1,0:T(8,128)(2,1)S(1)}, u32[]{:S(2)}, u32[]{:S(2)}) async-start(bf16[16,128,128]{2,1,0:T(8,128)(2,1)} %bitcast.11), calls=%async_computation | async-start | bytes 1048576 | tf_op jit(solution)/shard_map/all_to_all | solution.py:423
  18.6 14.3 %all-to-all-done = bf16[16,128,128]{2,1,0:T(8,128)(2,1)S(1)} async-done(((bf16[16,128,128]{2,1,0:T(8,128)(2,1)}), bf16[16,128,128]{2,1,0:T(8,128)(2,1)S(1)}, u32[]{:S(2)}, u32[]{:S(2)}) %all-to-all-start) | async-done | bytes 524320 | tf_op jit(solution)/shard_map/all_to_all | solution.py:423
  32.9 0.0 copy-start
  32.9 0.8 copy-done
  33.7 17.4 %shard_map.154 = (bf16[2048,128]{1,0:T(8,128)(2,1)}, f32[272,128]{1,0:T(8,128)}, bf16[272,128]{1,0:T(8,128)(2,1)}) custom-call(s32[1]{0:T(128)} %bitcast.core_ref, s32[2048]{0:T(1024)} %order_ref.4, bf16[2048,128]{1,0:T(8,128)(2,1)} %bitcast.9, bf16[2048,128]{1,0:T(8,128)(2,1)} %d_out_ref.1, f32[1,128]{1,0:T(1,128)} %bitcast.15, bf16[128,384]{1,0:T(8,128)(2,1)} %w_ref.4, ...), custom_call_target="tpu_custom_call" | custom-call | tf_op jit(solution)/shard_map/pallas_call | solution.py:371
  51.1 4.1 %all-to-all-start.1 = ((bf16[16,128,128]{2,1,0:T(8,128)(2,1)}), bf16[16,128,128]{2,1,0:T(8,128)(2,1)S(1)}, u32[]{:S(2)}, u32[]{:S(2)}) async-start(bf16[16,128,128]{2,1,0:T(8,128)(2,1)} %bitcast.12), calls=%async_computation.1 | async-start | bytes 1048576 | tf_op jit(solution)/shard_map/all_to_all | solution.py:423
  55.2 0.4 collective-permute-start
  55.6 1.1 %collective-permute-done = bf16[272,128]{1,0:T(8,128)(2,1)S(1)} collective-permute-done((bf16[272,128]{1,0:T(8,128)(2,1)}, bf16[272,128]{1,0:T(8,128)(2,1)S(1)}, u32[]{:S(2)}, u32[]{:S(2)}) %collective-permute-start) | collective-permute-done | bytes 69664 | tf_op jit(solution)/shard_map/ppermute | solution.py:427
  56.7 0.9 add_convert_fusion.5
  57.7 1.9 %collective-permute-start.1 = (bf16[272,128]{1,0:T(8,128)(2,1)S(1)}, bf16[272,128]{1,0:T(8,128)(2,1)S(1)}, u32[]{:S(2)}, u32[]{:S(2)}) collective-permute-start(bf16[272,128]{1,0:T(8,128)(2,1)S(1)} %add_convert_fusion.5), channel_id=1, source_target_pairs={{0,4},{2,6},{4,0},{6,2},{8,12},{10,14},{12,8},{14,10},{16,20},{18,... | collective-permute-start | bytes 208904 | tf_op jit(solution)/shard_map/ppermute | solution.py:427
  59.6 3.7 %collective-permute-done.1 = bf16[272,128]{1,0:T(8,128)(2,1)S(1)} collective-permute-done((bf16[272,128]{1,0:T(8,128)(2,1)S(1)}, bf16[272,128]{1,0:T(8,128)(2,1)S(1)}, u32[]{:S(2)}, u32[]{:S(2)}) %collective-permute-start.1) | collective-permute-done | bytes 69664 | tf_op jit(solution)/shard_map/ppermute | solution.py:427
  63.3 2.3 %collective-permute-start.2 = (bf16[272,128]{1,0:T(8,128)(2,1)S(1)}, bf16[272,128]{1,0:T(8,128)(2,1)S(1)}, u32[]{:S(2)}, u32[]{:S(2)}) collective-permute-start(bf16[272,128]{1,0:T(8,128)(2,1)S(1)} %add_convert_fusion.4), channel_id=1, source_target_pairs={{0,8},{2,10},{4,12},{6,14},{8,0},{10,2},{12,4},{14,6},{16,24},{18,... | collective-permute-start | bytes 208904 | tf_op jit(solution)/shard_map/ppermute | solution.py:427
  65.7 3.2 %collective-permute-done.2 = bf16[272,128]{1,0:T(8,128)(2,1)S(1)} collective-permute-done((bf16[272,128]{1,0:T(8,128)(2,1)S(1)}, bf16[272,128]{1,0:T(8,128)(2,1)S(1)}, u32[]{:S(2)}, u32[]{:S(2)}) %collective-permute-start.2) | collective-permute-done | bytes 69664 | tf_op jit(solution)/shard_map/ppermute | solution.py:427
  68.9 1.1 %all-to-all-done.1 = bf16[16,128,128]{2,1,0:T(8,128)(2,1)S(1)} async-done(((bf16[16,128,128]{2,1,0:T(8,128)(2,1)}), bf16[16,128,128]{2,1,0:T(8,128)(2,1)S(1)}, u32[]{:S(2)}, u32[]{:S(2)}) %all-to-all-start.1) | async-done | bytes 524320 | tf_op jit(solution)/shard_map/all_to_all | solution.py:423
  70.0 0.0 copy-start.1
  70.0 1.9 %collective-permute-start.3 = (bf16[272,128]{1,0:T(8,128)(2,1)S(1)}, bf16[272,128]{1,0:T(8,128)(2,1)S(1)}, u32[]{:S(2)}, u32[]{:S(2)}) collective-permute-start(bf16[272,128]{1,0:T(8,128)(2,1)S(1)} %convert_add_fusion.1), channel_id=1, source_target_pairs={{0,16},{2,18},{4,20},{6,22},{8,24},{10,26},{12,28},{14,30},{16,0},... | collective-permute-start | bytes 208904 | tf_op jit(solution)/shard_map/ppermute | solution.py:427
  71.9 0.0 copy-done.1
  71.9 14.2 %shard_map.155 = (bf16[2048,128]{1,0:T(8,128)(2,1)}, f32[272,128]{1,0:T(8,128)}, bf16[272,128]{1,0:T(8,128)(2,1)}) custom-call(s32[1]{0:T(128)} %bitcast.core_ref, s32[2048]{0:T(1024)} %order_ref.5, bf16[2048,128]{1,0:T(8,128)(2,1)} %bitcast.10, bf16[2048,128]{1,0:T(8,128)(2,1)} %x_ref.3, f32[1,128]{1,0:T(1,128)} %bitcast.14, bf16[128,384]{1,0:T(8,128)(2,1)} %w_ref.5, ...), custom_call_target="tpu_custom_call" | custom-call | tf_op jit(solution)/shard_map/pallas_call | solution.py:396
  86.2 0.0 collective-permute-done.3
  86.2 0.0 copy-start.2
  86.2 0.1 collective-permute-start.4
  86.3 1.5 %collective-permute-done.4 = bf16[272,128]{1,0:T(8,128)(2,1)S(1)} collective-permute-done((bf16[272,128]{1,0:T(8,128)(2,1)}, bf16[272,128]{1,0:T(8,128)(2,1)S(1)}, u32[]{:S(2)}, u32[]{:S(2)}) %collective-permute-start.4) | collective-permute-done | bytes 69664 | tf_op jit(solution)/shard_map/ppermute | solution.py:427
  87.8 0.9 add_convert_fusion.3
  88.7 0.4 collective-permute-start.5
  89.1 3.9 %collective-permute-done.5 = bf16[272,128]{1,0:T(8,128)(2,1)S(1)} collective-permute-done((bf16[272,128]{1,0:T(8,128)(2,1)S(1)}, bf16[272,128]{1,0:T(8,128)(2,1)S(1)}, u32[]{:S(2)}, u32[]{:S(2)}) %collective-permute-start.5) | collective-permute-done | bytes 69664 | tf_op jit(solution)/shard_map/ppermute | solution.py:427
  93.1 1.7 %collective-permute-start.6 = (bf16[272,128]{1,0:T(8,128)(2,1)S(1)}, bf16[272,128]{1,0:T(8,128)(2,1)S(1)}, u32[]{:S(2)}, u32[]{:S(2)}) collective-permute-start(bf16[272,128]{1,0:T(8,128)(2,1)S(1)} %add_convert_fusion.2), channel_id=1, source_target_pairs={{0,8},{2,10},{4,12},{6,14},{8,0},{10,2},{12,4},{14,6},{16,24},{18,... | collective-permute-start | bytes 208904 | tf_op jit(solution)/shard_map/ppermute | solution.py:427
  94.8 2.7 %collective-permute-done.6 = bf16[272,128]{1,0:T(8,128)(2,1)S(1)} collective-permute-done((bf16[272,128]{1,0:T(8,128)(2,1)S(1)}, bf16[272,128]{1,0:T(8,128)(2,1)S(1)}, u32[]{:S(2)}, u32[]{:S(2)}) %collective-permute-start.6) | collective-permute-done | bytes 69664 | tf_op jit(solution)/shard_map/ppermute | solution.py:427
  97.5 1.1 %collective-permute-start.7 = (bf16[272,128]{1,0:T(8,128)(2,1)S(1)}, bf16[272,128]{1,0:T(8,128)(2,1)S(1)}, u32[]{:S(2)}, u32[]{:S(2)}) collective-permute-start(bf16[272,128]{1,0:T(8,128)(2,1)S(1)} %add_convert_fusion.1), channel_id=1, source_target_pairs={{0,16},{2,18},{4,20},{6,22},{8,24},{10,26},{12,28},{14,30},{16,0},... | collective-permute-start | bytes 208904 | tf_op jit(solution)/shard_map/ppermute | solution.py:427
  98.6 0.0 collective-permute-start.9
  98.6 4.2 %collective-permute-done.7 = bf16[272,128]{1,0:T(8,128)(2,1)S(1)} collective-permute-done((bf16[272,128]{1,0:T(8,128)(2,1)S(1)}, bf16[272,128]{1,0:T(8,128)(2,1)S(1)}, u32[]{:S(2)}, u32[]{:S(2)}) %collective-permute-start.7) | collective-permute-done | bytes 69664 | tf_op jit(solution)/shard_map/ppermute | solution.py:427
  102.8 0.0 copy-start.3
  102.8 0.1 collective-permute-start.8
  102.9 0.0 collective-permute-done.9.came_b
  102.9 0.0 copy-start.4
  102.9 1.2 %collective-permute-done.8.came_a = bf16[272,128]{1,0:T(8,128)(2,1)S(1)} collective-permute-done((bf16[272,128]{1,0:T(8,128)(2,1)S(1)}, bf16[272,128]{1,0:T(8,128)(2,1)S(1)}, u32[]{:S(2)}, u32[]{:S(2)}) %collective-permute-start.8) | collective-permute-done | bytes 69664 | tf_op jit(solution)/shard_map/ppermute | solution.py:427
  104.1 0.0 copy-done.2
  104.1 0.0 copy-done.3
  104.1 0.0 copy-done.4
  104.1 0.0 copy-start.5
  104.2 0.6 copy-done.5
  104.8 1.8 %shard_map.156 = (f32[1,128]{1,0:T(1,128)}, f32[128,384]{1,0:T(8,128)}, f32[128,128]{1,0:T(8,128)}, f32[1,128]{1,0:T(1,128)}, f32[128,384]{1,0:T(8,128)}, /*index=5*/f32[128,128]{1,0:T(8,128)}) custom-call(s32[1]{0:T(128)} %bitcast.core_ref, bf16[272,128]{1,0:T(8,128)(2,1)} %copy-done.3, bf16[272,128]{1,0:T(8,128)(2,1)} %copy-done.5, ...), custom_call_target="tpu_custom_call" | custom-call | tf_op jit(solution)/shard_map/pallas_call | solution.py:414
  (6 shorter events, 0.1 us)
Async XLA Ops:
  11.0 21.9 %all-to-all-start = ((bf16[16,128,128]{2,1,0:T(8,128)(2,1)}), bf16[16,128,128]{2,1,0:T(8,128)(2,1)S(1)}, u32[]{:S(2)}, u32[]{:S(2)}) async-start(bf16[16,128,128]{2,1,0:T(8,128)(2,1)} %bitcast.11), calls=%async_computation | async-start | bytes 1048576 | tf_op jit(solution)/shard_map/all_to_all | solution.py:423
  32.9 0.8 copy-start
  51.1 18.9 %all-to-all-start.1 = ((bf16[16,128,128]{2,1,0:T(8,128)(2,1)}), bf16[16,128,128]{2,1,0:T(8,128)(2,1)S(1)}, u32[]{:S(2)}, u32[]{:S(2)}) async-start(bf16[16,128,128]{2,1,0:T(8,128)(2,1)} %bitcast.12), calls=%async_computation.1 | async-start | bytes 1048576 | tf_op jit(solution)/shard_map/all_to_all | solution.py:423
  55.2 1.5 %collective-permute-start = (bf16[272,128]{1,0:T(8,128)(2,1)}, bf16[272,128]{1,0:T(8,128)(2,1)S(1)}, u32[]{:S(2)}, u32[]{:S(2)}) collective-permute-start(bf16[272,128]{1,0:T(8,128)(2,1)} %get-tuple-element.32), channel_id=1, source_target_pairs={{0,2},{2,0},{4,6},{6,4},{8,10},{10,8},{12,14},{14,12},{16,18},{18,... | collective-permute-start | bytes 208904 | tf_op jit(solution)/shard_map/ppermute | solution.py:427
  57.7 5.6 %collective-permute-start.1 = (bf16[272,128]{1,0:T(8,128)(2,1)S(1)}, bf16[272,128]{1,0:T(8,128)(2,1)S(1)}, u32[]{:S(2)}, u32[]{:S(2)}) collective-permute-start(bf16[272,128]{1,0:T(8,128)(2,1)S(1)} %add_convert_fusion.5), channel_id=1, source_target_pairs={{0,4},{2,6},{4,0},{6,2},{8,12},{10,14},{12,8},{14,10},{16,20},{18,... | collective-permute-start | bytes 208904 | tf_op jit(solution)/shard_map/ppermute | solution.py:427
  63.3 5.6 %collective-permute-start.2 = (bf16[272,128]{1,0:T(8,128)(2,1)S(1)}, bf16[272,128]{1,0:T(8,128)(2,1)S(1)}, u32[]{:S(2)}, u32[]{:S(2)}) collective-permute-start(bf16[272,128]{1,0:T(8,128)(2,1)S(1)} %add_convert_fusion.4), channel_id=1, source_target_pairs={{0,8},{2,10},{4,12},{6,14},{8,0},{10,2},{12,4},{14,6},{16,24},{18,... | collective-permute-start | bytes 208904 | tf_op jit(solution)/shard_map/ppermute | solution.py:427
  70.0 1.9 %copy-start.1 = (bf16[16,128,128]{2,1,0:T(8,128)(2,1)}, bf16[16,128,128]{2,1,0:T(8,128)(2,1)S(1)}, u32[]{:S(2)}) copy-start(bf16[16,128,128]{2,1,0:T(8,128)(2,1)S(1)} %all-to-all-done.1) | copy-start | bytes 1572868
  70.0 16.1 %collective-permute-start.3 = (bf16[272,128]{1,0:T(8,128)(2,1)S(1)}, bf16[272,128]{1,0:T(8,128)(2,1)S(1)}, u32[]{:S(2)}, u32[]{:S(2)}) collective-permute-start(bf16[272,128]{1,0:T(8,128)(2,1)S(1)} %convert_add_fusion.1), channel_id=1, source_target_pairs={{0,16},{2,18},{4,20},{6,22},{8,24},{10,26},{12,28},{14,30},{16,0},... | collective-permute-start | bytes 208904 | tf_op jit(solution)/shard_map/ppermute | solution.py:427
  86.2 17.9 %copy-start.2 = (bf16[272,128]{1,0:T(8,128)(2,1)}, bf16[272,128]{1,0:T(8,128)(2,1)S(1)}, u32[]{:S(2)}) copy-start(bf16[272,128]{1,0:T(8,128)(2,1)S(1)} %convert_add_fusion.mine_b) | copy-start | bytes 208900
  86.2 1.5 %collective-permute-start.4 = (bf16[272,128]{1,0:T(8,128)(2,1)}, bf16[272,128]{1,0:T(8,128)(2,1)S(1)}, u32[]{:S(2)}, u32[]{:S(2)}) collective-permute-start(bf16[272,128]{1,0:T(8,128)(2,1)} %get-tuple-element.43), channel_id=1, source_target_pairs={{0,2},{2,0},{4,6},{6,4},{8,10},{10,8},{12,14},{14,12},{16,18},{18,... | collective-permute-start | bytes 208904 | tf_op jit(solution)/shard_map/ppermute | solution.py:427
  88.7 4.4 %collective-permute-start.5 = (bf16[272,128]{1,0:T(8,128)(2,1)S(1)}, bf16[272,128]{1,0:T(8,128)(2,1)S(1)}, u32[]{:S(2)}, u32[]{:S(2)}) collective-permute-start(bf16[272,128]{1,0:T(8,128)(2,1)S(1)} %add_convert_fusion.3), channel_id=1, source_target_pairs={{0,4},{2,6},{4,0},{6,2},{8,12},{10,14},{12,8},{14,10},{16,20},{18,... | collective-permute-start | bytes 208904 | tf_op jit(solution)/shard_map/ppermute | solution.py:427
  93.1 4.4 %collective-permute-start.6 = (bf16[272,128]{1,0:T(8,128)(2,1)S(1)}, bf16[272,128]{1,0:T(8,128)(2,1)S(1)}, u32[]{:S(2)}, u32[]{:S(2)}) collective-permute-start(bf16[272,128]{1,0:T(8,128)(2,1)S(1)} %add_convert_fusion.2), channel_id=1, source_target_pairs={{0,8},{2,10},{4,12},{6,14},{8,0},{10,2},{12,4},{14,6},{16,24},{18,... | collective-permute-start | bytes 208904 | tf_op jit(solution)/shard_map/ppermute | solution.py:427
  97.5 5.3 %collective-permute-start.7 = (bf16[272,128]{1,0:T(8,128)(2,1)S(1)}, bf16[272,128]{1,0:T(8,128)(2,1)S(1)}, u32[]{:S(2)}, u32[]{:S(2)}) collective-permute-start(bf16[272,128]{1,0:T(8,128)(2,1)S(1)} %add_convert_fusion.1), channel_id=1, source_target_pairs={{0,16},{2,18},{4,20},{6,22},{8,24},{10,26},{12,28},{14,30},{16,0},... | collective-permute-start | bytes 208904 | tf_op jit(solution)/shard_map/ppermute | solution.py:427
  98.6 4.3 %collective-permute-start.9 = (bf16[272,128]{1,0:T(8,128)(2,1)S(1)}, bf16[272,128]{1,0:T(8,128)(2,1)S(1)}, u32[]{:S(2)}, u32[]{:S(2)}) collective-permute-start(bf16[272,128]{1,0:T(8,128)(2,1)S(1)} %convert_add_fusion.mine_b), channel_id=1, source_target_pairs={{0,2},{2,0},{4,6},{6,4},{8,10},{10,8},{12,14},{14,12},{16,18},{18,... | collective-permute-start | bytes 208904 | tf_op jit(solution)/shard_map/ppermute | solution.py:427
  102.8 1.3 %copy-start.3 = (bf16[272,128]{1,0:T(8,128)(2,1)}, bf16[272,128]{1,0:T(8,128)(2,1)S(1)}, u32[]{:S(2)}) copy-start(bf16[272,128]{1,0:T(8,128)(2,1)S(1)} %add_convert_fusion.mine_a) | copy-start | bytes 208900
  102.8 1.3 %collective-permute-start.8 = (bf16[272,128]{1,0:T(8,128)(2,1)S(1)}, bf16[272,128]{1,0:T(8,128)(2,1)S(1)}, u32[]{:S(2)}, u32[]{:S(2)}) collective-permute-start(bf16[272,128]{1,0:T(8,128)(2,1)S(1)} %add_convert_fusion.mine_a), channel_id=1, source_target_pairs={{0,2},{2,0},{4,6},{6,4},{8,10},{10,8},{12,14},{14,12},{16,18},{18,... | collective-permute-start | bytes 208904 | tf_op jit(solution)/shard_map/ppermute | solution.py:427
  102.9 1.2 %copy-start.4 = (bf16[272,128]{1,0:T(8,128)(2,1)}, bf16[272,128]{1,0:T(8,128)(2,1)S(1)}, u32[]{:S(2)}) copy-start(bf16[272,128]{1,0:T(8,128)(2,1)S(1)} %collective-permute-done.9.came_b) | copy-start | bytes 208900
  104.1 0.6 copy-start.5

commit v4 on v3

--- a/solution.py
+++ b/solution.py
@@ -14,7 +14,8 @@
 LN2 = 0.6931471805599453
 SCALE = HEAD_DIM ** (-0.5)
 VMEM_LIMIT = 56 * 1024 * 1024
-UNROLL = 32
+SMALL_LIMIT = 16 * 1024 * 1024
+UNROLL = 128
 AHEAD = 3
 CHUNK = BALL // HEADS
 GRAD_HALF = 2 * D + 16
@@ -222,10 +223,10 @@
     staggered(
         heads,
         (0, at_first(prepare)),
-        (2, forward.score),
+        (3, forward.score),
         (6, forward.soften),
-        (8, forward.attend),
-        (8, at_last(finish)),
+        (9, forward.attend),
+        (13, at_last(finish)),
     )
     gather(order_ref, out, sent)
     sent_ref[...] = sent[...].astype(bf16)
@@ -263,12 +264,12 @@
         (14, forward.soften),
         (16, forward.attend),
         (16, at_last(join)),
+        (25, backward.value),
         (25, backward.weigh),
-        (28, backward.score),
-        (28, backward.value),
-        (30, backward.query_key),
-        (30, at_last(finish)),
-        (39, lambda i: scatter_chunk(i, order_ref, d_in, d_came)),
+        (27, backward.score),
+        (29, backward.query_key),
+        (31, at_last(finish)),
+        (41, lambda i: scatter_chunk(i, order_ref, d_in, d_came)),
     )
     sent_ref[...] = d_came[...].astype(bf16)
     share(core_ref, sums, halves, mine_ref, other_ref)
@@ -304,11 +305,11 @@
     staggered(
         balls * HEADS,
         (0, at_first(prepare)),
-        (2, backward.weigh),
-        (5, backward.score),
-        (5, backward.value),
-        (7, backward.query_key),
-        (7, at_last(finish)),
+        (4, backward.value),
+        (4, backward.weigh),
+        (7, backward.score),
+        (10, backward.query_key),
+        (13, at_last(finish)),
     )
     share(core_ref, sums, halves, mine_ref, other_ref)
 
@@ -338,14 +339,14 @@
 REMAIN = pl.BlockSpec(memory_space=pl.ANY)
 
 
-def call(kernel, in_specs, outs, scratch):
+def call(kernel, in_specs, outs, scratch, limit=VMEM_LIMIT):
     return pl.pallas_call(
         kernel,
         in_specs=in_specs,
         out_specs=[spec for spec, _, _ in outs],
         out_shape=[jax.ShapeDtypeStruct(shape, kind) for _, shape, kind in outs],
         scratch_shapes=scratch,
-        compiler_params=pltpu.CompilerParams(vmem_limit_bytes=VMEM_LIMIT),
+        compiler_params=pltpu.CompilerParams(vmem_limit_bytes=limit),
     )
 
 
@@ -416,6 +417,7 @@
         [SCALARS] + [REMAIN] * 4,
         [(VECTORS, shape, f32) for shape in shapes],
         [pltpu.VMEM((GRAD_HALF, D), bf16)] * 4 + [pltpu.SemaphoreType.DMA((4,))],
+        SMALL_LIMIT,
     )(core, *parts)
 
 
@@ -446,6 +448,7 @@
 
 def body(tokens, cotangent, order_send, order_recv, gain_a, qkv_a, proj_a, gain_b, qkv_b, proj_b):
     core = (lax.axis_index("wide") % 2).astype(jnp.int32).reshape(1)
+    order_send, core = lax.optimization_barrier((order_send, core))
     gain_a = gain_a.reshape(1, D)
     gain_b = gain_b.reshape(1, D)
     sent, inv, *kept = first_call(order_send, tokens, gain_a, qkv_a, proj_a)

time: 107 us -> 101 us (0.944)
  blocking collectives: 0 us -> 22 us
  waiting for transfers between devices: 37 us -> 22.7 us
  starting transfers between devices: 21.6 us -> 14 us
  Pallas kernels: 43.8 us -> 38.8 us
  local copies, waits for them, and re-layouts: 1.42 us -> 0.01 us
    all_to_all x0 -> x1, blocking collectives: none -> 22 us  [exchange(): return lax.all_to_all(rows, 'wide', split_axis=0, concat_axis=0, tiled=True)]
    all_to_all x2 -> x1, waiting for transfers between devices: 15.4 us -> 1.13 us  [exchange(): return lax.all_to_all(rows, 'wide', split_axis=0, concat_axis=0, tiled=True)]
    all_to_all x2 -> x1, starting transfers between devices: 11.7 us -> 4.09 us  [exchange(): return lax.all_to_all(rows, 'wide', split_axis=0, concat_axis=0, tiled=True)]
    pallas_call x1, Pallas kernels: 17.4 us -> 15.5 us  [second_call(): call(second_kernel, [SCALARS] * 2 + [VECTORS] * 5, [(VECTORS, (rows, D),...]
    pallas_call x1, Pallas kernels: 10.4 us -> 8.94 us  [first_call(): call(first_kernel, [SCALARS] + [VECTORS] * 4, [(VECTORS, (rows, D), bf16)...]
    unnamed x12 -> x2, local copies, waits for them, and re-layouts: 1.42 us -> 0.01 us
    pallas_call x1, Pallas kernels: 14.2 us -> 13.1 us  [third_call(): call(third_kernel, [SCALARS] * 2 + [VECTORS] * 6 + [REMAIN] * 3, [(VECTOR...]
  transfers between devices with their start and end apart: 12 -> 11, of which waited for: 10 -> 9; matrix products, arithmetic and copies ran while one was open for 1% -> 1% of each run, Pallas kernels for 13% -> 13%
where the time goes in v4:
time: 101 us; the launch traced here: 100 us
  Pallas kernels  38.8 us (38%)
  waiting for transfers between devices  22.7 us (22%)
  blocking collectives  22 us (22%)
  starting transfers between devices  14 us (14%)
  other arithmetic  1.99 us (2%)
    all_to_all x1, blocking collectives, exchange(): return lax.all_to_all(rows, 'wide', split_axis=0, concat_axis=0, tiled=True)  22 us
    ppermute x10, waiting for transfers between devices, swap(): return lax.ppermute(part, 'wide', [(i, i ^ apart) for i in range(peers)])  21.6 us
    pallas_call x1, Pallas kernels, second_call(): call(second_kernel, [SCALARS] * 2 + [VECTORS] * 5, [(VECTORS, (rows, D),...  15.5 us
    pallas_call x1, Pallas kernels, third_call(): call(third_kernel, [SCALARS] * 2 + [VECTORS] * 6 + [REMAIN] * 3, [(VECTOR...  13.1 us
    ppermute x10, starting transfers between devices, swap(): return lax.ppermute(part, 'wide', [(i, i ^ apart) for i in range(peers)])  9.92 us
    pallas_call x1, Pallas kernels, first_call(): call(first_kernel, [SCALARS] + [VECTORS] * 4, [(VECTORS, (rows, D), bf16)...  8.94 us
    all_to_all x1, starting transfers between devices, exchange(): return lax.all_to_all(rows, 'wide', split_axis=0, concat_axis=0, tiled=True)  4.09 us
  transfers between devices with their start and end apart: 11, of which 9 were waited for; matrix products, arithmetic and copies ran while one was open for 1% of the time, Pallas kernels for 13%

profile of v4, /device:TPU:0, one launch (start us, length us, event | category | flops | bytes accessed | tf_op | source)
XLA Modules:
  0.0 100.4 jit_solution(18444963264239111623)
XLA Ops:
  0.6 8.9 %shard_map.153 = (bf16[2048,128]{1,0:T(8,128)(2,1)}, f32[8,8,256]{2,1,0:T(8,128)}, bf16[8,8,256,256]{3,2,1,0:T(8,128)(2,1)}, bf16[8,384,256]{2,1,0:T(8,128)(2,1)}, bf16[8,256,128]{2,1,0:T(8,128)(2,1)}) custom-call(s32[2048]{0:T(1024)} %order_ref.3, bf16[2048,128]{1,0:T(8,128)(2,1)} %x_ref.3, f32[1,128]{1,0:T(1,128)} %bitcast.13, bf16[128,384]{1,0:T(8,128)(2,1)} %w_ref.5, ...), custom_call_target="tpu_custom_call" | custom-call | tf_op jit(solution)/shard_map/pallas_call | solution.py:357
  9.6 22.0 %all_to_all.23 = bf16[16,128,128]{2,1,0:T(8,128)(2,1)} all-to-all(bf16[16,128,128]{2,1,0:T(8,128)(2,1)} %bitcast.12), channel_id=1, replica_groups=mesh['wide'=16,'grp'=2] {'wide'}, dimensions={0} | all-to-all | bytes 1048576 | tf_op jit(solution)/shard_map/all_to_all | solution.py:425
  31.6 15.5 %shard_map.154 = (bf16[2048,128]{1,0:T(8,128)(2,1)}, f32[272,128]{1,0:T(8,128)}, bf16[272,128]{1,0:T(8,128)(2,1)}) custom-call(s32[1]{0:T(128)} %bitcast.core_ref, s32[2048]{0:T(1024)} %order_ref.2, bf16[2048,128]{1,0:T(8,128)(2,1)} %bitcast.9, bf16[2048,128]{1,0:T(8,128)(2,1)} %d_out_ref.1, f32[1,128]{1,0:T(1,128)} %bitcast.15, bf16[128,384]{1,0:T(8,128)(2,1)} %w_ref.4, ...), custom_call_target="tpu_custom_call" | custom-call | tf_op jit(solution)/shard_map/pallas_call | solution.py:372
  47.1 4.1 %all-to-all-start.1 = ((bf16[16,128,128]{2,1,0:T(8,128)(2,1)}), bf16[16,128,128]{2,1,0:T(8,128)(2,1)S(1)}, u32[]{:S(2)}, u32[]{:S(2)}) async-start(bf16[16,128,128]{2,1,0:T(8,128)(2,1)} %bitcast.11), calls=%async_computation.1 | async-start | bytes 1048576 | tf_op jit(solution)/shard_map/all_to_all | solution.py:425
  51.2 0.4 collective-permute-start
  51.6 1.1 %collective-permute-done = bf16[272,128]{1,0:T(8,128)(2,1)S(1)} collective-permute-done((bf16[272,128]{1,0:T(8,128)(2,1)}, bf16[272,128]{1,0:T(8,128)(2,1)S(1)}, u32[]{:S(2)}, u32[]{:S(2)}) %collective-permute-start) | collective-permute-done | bytes 69664 | tf_op jit(solution)/shard_map/ppermute | solution.py:429
  52.7 0.9 add_convert_fusion.5
  53.6 1.9 %collective-permute-start.1 = (bf16[272,128]{1,0:T(8,128)(2,1)S(1)}, bf16[272,128]{1,0:T(8,128)(2,1)S(1)}, u32[]{:S(2)}, u32[]{:S(2)}) collective-permute-start(bf16[272,128]{1,0:T(8,128)(2,1)S(1)} %add_convert_fusion.5), channel_id=1, source_target_pairs={{0,4},{2,6},{4,0},{6,2},{8,12},{10,14},{12,8},{14,10},{16,20},{18,... | collective-permute-start | bytes 208904 | tf_op jit(solution)/shard_map/ppermute | solution.py:429
  55.6 3.7 %collective-permute-done.1 = bf16[272,128]{1,0:T(8,128)(2,1)S(1)} collective-permute-done((bf16[272,128]{1,0:T(8,128)(2,1)S(1)}, bf16[272,128]{1,0:T(8,128)(2,1)S(1)}, u32[]{:S(2)}, u32[]{:S(2)}) %collective-permute-start.1) | collective-permute-done | bytes 69664 | tf_op jit(solution)/shard_map/ppermute | solution.py:429
  59.3 2.3 %collective-permute-start.2 = (bf16[272,128]{1,0:T(8,128)(2,1)S(1)}, bf16[272,128]{1,0:T(8,128)(2,1)S(1)}, u32[]{:S(2)}, u32[]{:S(2)}) collective-permute-start(bf16[272,128]{1,0:T(8,128)(2,1)S(1)} %add_convert_fusion.4), channel_id=1, source_target_pairs={{0,8},{2,10},{4,12},{6,14},{8,0},{10,2},{12,4},{14,6},{16,24},{18,... | collective-permute-start | bytes 208904 | tf_op jit(solution)/shard_map/ppermute | solution.py:429
  61.6 3.2 %collective-permute-done.2 = bf16[272,128]{1,0:T(8,128)(2,1)S(1)} collective-permute-done((bf16[272,128]{1,0:T(8,128)(2,1)S(1)}, bf16[272,128]{1,0:T(8,128)(2,1)S(1)}, u32[]{:S(2)}, u32[]{:S(2)}) %collective-permute-start.2) | collective-permute-done | bytes 69664 | tf_op jit(solution)/shard_map/ppermute | solution.py:429
  64.9 1.1 %all-to-all-done.1 = bf16[16,128,128]{2,1,0:T(8,128)(2,1)S(1)} async-done(((bf16[16,128,128]{2,1,0:T(8,128)(2,1)}), bf16[16,128,128]{2,1,0:T(8,128)(2,1)S(1)}, u32[]{:S(2)}, u32[]{:S(2)}) %all-to-all-start.1) | async-done | bytes 524320 | tf_op jit(solution)/shard_map/all_to_all | solution.py:425
  66.0 0.0 copy-start
  66.0 1.9 %collective-permute-start.3 = (bf16[272,128]{1,0:T(8,128)(2,1)S(1)}, bf16[272,128]{1,0:T(8,128)(2,1)S(1)}, u32[]{:S(2)}, u32[]{:S(2)}) collective-permute-start(bf16[272,128]{1,0:T(8,128)(2,1)S(1)} %convert_add_fusion.1), channel_id=1, source_target_pairs={{0,16},{2,18},{4,20},{6,22},{8,24},{10,26},{12,28},{14,30},{16,0},... | collective-permute-start | bytes 208904 | tf_op jit(solution)/shard_map/ppermute | solution.py:429
  67.9 0.0 copy-done
  67.9 13.1 %shard_map.155 = (bf16[2048,128]{1,0:T(8,128)(2,1)}, f32[272,128]{1,0:T(8,128)}, bf16[272,128]{1,0:T(8,128)(2,1)}) custom-call(s32[1]{0:T(128)} %bitcast.core_ref, s32[2048]{0:T(1024)} %order_ref.3, bf16[2048,128]{1,0:T(8,128)(2,1)} %bitcast.10, bf16[2048,128]{1,0:T(8,128)(2,1)} %x_ref.3, f32[1,128]{1,0:T(1,128)} %bitcast.14, bf16[128,384]{1,0:T(8,128)(2,1)} %w_ref.5, ...), custom_call_target="tpu_custom_call" | custom-call | tf_op jit(solution)/shard_map/pallas_call | solution.py:397
  81.1 0.0 collective-permute-done.3
  81.1 0.1 collective-permute-start.4
  81.2 1.5 %collective-permute-done.4 = bf16[272,128]{1,0:T(8,128)(2,1)S(1)} collective-permute-done((bf16[272,128]{1,0:T(8,128)(2,1)}, bf16[272,128]{1,0:T(8,128)(2,1)S(1)}, u32[]{:S(2)}, u32[]{:S(2)}) %collective-permute-start.4) | collective-permute-done | bytes 69664 | tf_op jit(solution)/shard_map/ppermute | solution.py:429
  82.6 0.9 add_convert_fusion.3
  83.6 0.4 collective-permute-start.5
  84.0 3.9 %collective-permute-done.5 = bf16[272,128]{1,0:T(8,128)(2,1)S(1)} collective-permute-done((bf16[272,128]{1,0:T(8,128)(2,1)S(1)}, bf16[272,128]{1,0:T(8,128)(2,1)S(1)}, u32[]{:S(2)}, u32[]{:S(2)}) %collective-permute-start.5) | collective-permute-done | bytes 69664 | tf_op jit(solution)/shard_map/ppermute | solution.py:429
  88.0 1.7 %collective-permute-start.6 = (bf16[272,128]{1,0:T(8,128)(2,1)S(1)}, bf16[272,128]{1,0:T(8,128)(2,1)S(1)}, u32[]{:S(2)}, u32[]{:S(2)}) collective-permute-start(bf16[272,128]{1,0:T(8,128)(2,1)S(1)} %add_convert_fusion.2), channel_id=1, source_target_pairs={{0,8},{2,10},{4,12},{6,14},{8,0},{10,2},{12,4},{14,6},{16,24},{18,... | collective-permute-start | bytes 208904 | tf_op jit(solution)/shard_map/ppermute | solution.py:429
  89.6 2.7 %collective-permute-done.6 = bf16[272,128]{1,0:T(8,128)(2,1)S(1)} collective-permute-done((bf16[272,128]{1,0:T(8,128)(2,1)S(1)}, bf16[272,128]{1,0:T(8,128)(2,1)S(1)}, u32[]{:S(2)}, u32[]{:S(2)}) %collective-permute-start.6) | collective-permute-done | bytes 69664 | tf_op jit(solution)/shard_map/ppermute | solution.py:429
  92.4 1.1 %collective-permute-start.7 = (bf16[272,128]{1,0:T(8,128)(2,1)S(1)}, bf16[272,128]{1,0:T(8,128)(2,1)S(1)}, u32[]{:S(2)}, u32[]{:S(2)}) collective-permute-start(bf16[272,128]{1,0:T(8,128)(2,1)S(1)} %add_convert_fusion.1), channel_id=1, source_target_pairs={{0,16},{2,18},{4,20},{6,22},{8,24},{10,26},{12,28},{14,30},{16,0},... | collective-permute-start | bytes 208904 | tf_op jit(solution)/shard_map/ppermute | solution.py:429
  93.5 0.0 collective-permute-start.9
  93.5 4.2 %collective-permute-done.7 = bf16[272,128]{1,0:T(8,128)(2,1)S(1)} collective-permute-done((bf16[272,128]{1,0:T(8,128)(2,1)S(1)}, bf16[272,128]{1,0:T(8,128)(2,1)S(1)}, u32[]{:S(2)}, u32[]{:S(2)}) %collective-permute-start.7) | collective-permute-done | bytes 69664 | tf_op jit(solution)/shard_map/ppermute | solution.py:429
  97.7 0.1 collective-permute-start.8
  97.8 0.0 collective-permute-done.9.came_b
  97.8 1.2 %collective-permute-done.8.came_a = bf16[272,128]{1,0:T(8,128)(2,1)S(1)} collective-permute-done((bf16[272,128]{1,0:T(8,128)(2,1)S(1)}, bf16[272,128]{1,0:T(8,128)(2,1)S(1)}, u32[]{:S(2)}, u32[]{:S(2)}) %collective-permute-start.8) | collective-permute-done | bytes 69664 | tf_op jit(solution)/shard_map/ppermute | solution.py:429
  99.0 1.2 %shard_map.156 = (f32[1,128]{1,0:T(1,128)}, f32[128,384]{1,0:T(8,128)}, f32[128,128]{1,0:T(8,128)}, f32[1,128]{1,0:T(1,128)}, f32[128,384]{1,0:T(8,128)}, /*index=5*/f32[128,128]{1,0:T(8,128)}) custom-call(s32[1]{0:T(128)} %bitcast.core_ref, bf16[272,128]{1,0:T(8,128)(2,1)S(1)} %add_convert_fusion.mine_a, ...), custom_call_target="tpu_custom_call" | custom-call | tf_op jit(solution)/shard_map/pallas_call | solution.py:415
  (6 shorter events, 0.1 us)
Async XLA Ops:
  47.1 18.9 %all-to-all-start.1 = ((bf16[16,128,128]{2,1,0:T(8,128)(2,1)}), bf16[16,128,128]{2,1,0:T(8,128)(2,1)S(1)}, u32[]{:S(2)}, u32[]{:S(2)}) async-start(bf16[16,128,128]{2,1,0:T(8,128)(2,1)} %bitcast.11), calls=%async_computation.1 | async-start | bytes 1048576 | tf_op jit(solution)/shard_map/all_to_all | solution.py:425
  51.2 1.5 %collective-permute-start = (bf16[272,128]{1,0:T(8,128)(2,1)}, bf16[272,128]{1,0:T(8,128)(2,1)S(1)}, u32[]{:S(2)}, u32[]{:S(2)}) collective-permute-start(bf16[272,128]{1,0:T(8,128)(2,1)} %get-tuple-element.36), channel_id=1, source_target_pairs={{0,2},{2,0},{4,6},{6,4},{8,10},{10,8},{12,14},{14,12},{16,18},{18,... | collective-permute-start | bytes 208904 | tf_op jit(solution)/shard_map/ppermute | solution.py:429
  53.6 5.6 %collective-permute-start.1 = (bf16[272,128]{1,0:T(8,128)(2,1)S(1)}, bf16[272,128]{1,0:T(8,128)(2,1)S(1)}, u32[]{:S(2)}, u32[]{:S(2)}) collective-permute-start(bf16[272,128]{1,0:T(8,128)(2,1)S(1)} %add_convert_fusion.5), channel_id=1, source_target_pairs={{0,4},{2,6},{4,0},{6,2},{8,12},{10,14},{12,8},{14,10},{16,20},{18,... | collective-permute-start | bytes 208904 | tf_op jit(solution)/shard_map/ppermute | solution.py:429
  59.3 5.6 %collective-permute-start.2 = (bf16[272,128]{1,0:T(8,128)(2,1)S(1)}, bf16[272,128]{1,0:T(8,128)(2,1)S(1)}, u32[]{:S(2)}, u32[]{:S(2)}) collective-permute-start(bf16[272,128]{1,0:T(8,128)(2,1)S(1)} %add_convert_fusion.4), channel_id=1, source_target_pairs={{0,8},{2,10},{4,12},{6,14},{8,0},{10,2},{12,4},{14,6},{16,24},{18,... | collective-permute-start | bytes 208904 | tf_op jit(solution)/shard_map/ppermute | solution.py:429
  66.0 1.9 %copy-start = (bf16[16,128,128]{2,1,0:T(8,128)(2,1)}, bf16[16,128,128]{2,1,0:T(8,128)(2,1)S(1)}, u32[]{:S(2)}) copy-start(bf16[16,128,128]{2,1,0:T(8,128)(2,1)S(1)} %all-to-all-done.1) | copy-start | bytes 1572868
  66.0 15.0 %collective-permute-start.3 = (bf16[272,128]{1,0:T(8,128)(2,1)S(1)}, bf16[272,128]{1,0:T(8,128)(2,1)S(1)}, u32[]{:S(2)}, u32[]{:S(2)}) collective-permute-start(bf16[272,128]{1,0:T(8,128)(2,1)S(1)} %convert_add_fusion.1), channel_id=1, source_target_pairs={{0,16},{2,18},{4,20},{6,22},{8,24},{10,26},{12,28},{14,30},{16,0},... | collective-permute-start | bytes 208904 | tf_op jit(solution)/shard_map/ppermute | solution.py:429
  81.1 1.5 %collective-permute-start.4 = (bf16[272,128]{1,0:T(8,128)(2,1)}, bf16[272,128]{1,0:T(8,128)(2,1)S(1)}, u32[]{:S(2)}, u32[]{:S(2)}) collective-permute-start(bf16[272,128]{1,0:T(8,128)(2,1)} %get-tuple-element.47), channel_id=1, source_target_pairs={{0,2},{2,0},{4,6},{6,4},{8,10},{10,8},{12,14},{14,12},{16,18},{18,... | collective-permute-start | bytes 208904 | tf_op jit(solution)/shard_map/ppermute | solution.py:429
  83.6 4.4 %collective-permute-start.5 = (bf16[272,128]{1,0:T(8,128)(2,1)S(1)}, bf16[272,128]{1,0:T(8,128)(2,1)S(1)}, u32[]{:S(2)}, u32[]{:S(2)}) collective-permute-start(bf16[272,128]{1,0:T(8,128)(2,1)S(1)} %add_convert_fusion.3), channel_id=1, source_target_pairs={{0,4},{2,6},{4,0},{6,2},{8,12},{10,14},{12,8},{14,10},{16,20},{18,... | collective-permute-start | bytes 208904 | tf_op jit(solution)/shard_map/ppermute | solution.py:429
  88.0 4.4 %collective-permute-start.6 = (bf16[272,128]{1,0:T(8,128)(2,1)S(1)}, bf16[272,128]{1,0:T(8,128)(2,1)S(1)}, u32[]{:S(2)}, u32[]{:S(2)}) collective-permute-start(bf16[272,128]{1,0:T(8,128)(2,1)S(1)} %add_convert_fusion.2), channel_id=1, source_target_pairs={{0,8},{2,10},{4,12},{6,14},{8,0},{10,2},{12,4},{14,6},{16,24},{18,... | collective-permute-start | bytes 208904 | tf_op jit(solution)/shard_map/ppermute | solution.py:429
  92.4 5.3 %collective-permute-start.7 = (bf16[272,128]{1,0:T(8,128)(2,1)S(1)}, bf16[272,128]{1,0:T(8,128)(2,1)S(1)}, u32[]{:S(2)}, u32[]{:S(2)}) collective-permute-start(bf16[272,128]{1,0:T(8,128)(2,1)S(1)} %add_convert_fusion.1), channel_id=1, source_target_pairs={{0,16},{2,18},{4,20},{6,22},{8,24},{10,26},{12,28},{14,30},{16,0},... | collective-permute-start | bytes 208904 | tf_op jit(solution)/shard_map/ppermute | solution.py:429
  93.5 4.3 %collective-permute-start.9 = (bf16[272,128]{1,0:T(8,128)(2,1)S(1)}, bf16[272,128]{1,0:T(8,128)(2,1)S(1)}, u32[]{:S(2)}, u32[]{:S(2)}) collective-permute-start(bf16[272,128]{1,0:T(8,128)(2,1)S(1)} %convert_add_fusion.mine_b), channel_id=1, source_target_pairs={{0,2},{2,0},{4,6},{6,4},{8,10},{10,8},{12,14},{14,12},{16,18},{18,... | collective-permute-start | bytes 208904 | tf_op jit(solution)/shard_map/ppermute | solution.py:429
  97.7 1.3 %collective-permute-start.8 = (bf16[272,128]{1,0:T(8,128)(2,1)S(1)}, bf16[272,128]{1,0:T(8,128)(2,1)S(1)}, u32[]{:S(2)}, u32[]{:S(2)}) collective-permute-start(bf16[272,128]{1,0:T(8,128)(2,1)S(1)} %add_convert_fusion.mine_a), channel_id=1, source_target_pairs={{0,2},{2,0},{4,6},{6,4},{8,10},{10,8},{12,14},{14,12},{16,18},{18,... | collective-permute-start | bytes 208904 | tf_op jit(solution)/shard_map/ppermute | solution.py:429

commit v5 on v4

--- a/solution.py
+++ b/solution.py
@@ -108,14 +108,14 @@
 
     def weigh(self, i):
         ball, h = divmod(i, HEADS)
-        self.d_weights[i] = dot(self.parts[ball][2] * head_mask(h), self.d_att[ball])
+        self.d_weights[i] = dot(self.parts[ball][2] * head_mask(h), self.d_att[ball]).astype(bf16)
 
     def score(self, i):
         ball, h = divmod(i, HEADS)
         own = self.d_att[ball][rows_of(h)]
         att = self.att_ref[ball, rows_of(h), :]
         delta = jnp.sum(own.astype(f32) * att.astype(f32), axis=0, keepdims=True)
-        self.d_s[ball, h] = (self.e_ref[ball, h].astype(f32) * (self.d_weights.pop(i) - delta)).astype(bf16)
+        self.d_s[ball, h] = (self.e_ref[ball, h].astype(f32) * (self.d_weights.pop(i).astype(f32) - delta)).astype(bf16)
 
     def put(self, part, ball, h, value):
         start = part * D + h * HEAD_DIM
@@ -223,10 +223,10 @@
     staggered(
         heads,
         (0, at_first(prepare)),
-        (3, forward.score),
-        (6, forward.soften),
-        (9, forward.attend),
-        (13, at_last(finish)),
+        (4, forward.score),
+        (8, forward.soften),
+        (12, forward.attend),
+        (17, at_last(finish)),
     )
     gather(order_ref, out, sent)
     sent_ref[...] = sent[...].astype(bf16)

time: 101 us -> 101 us (level)
  no operation moved by 1% of the time
where the time goes in v5:
time: 101 us; the launch traced here: 100 us
  Pallas kernels  38.6 us (38%)
  waiting for transfers between devices  22.7 us (22%)
  blocking collectives  22 us (22%)
  starting transfers between devices  14 us (14%)
  other arithmetic  1.99 us (2%)
    all_to_all x1, blocking collectives, exchange(): return lax.all_to_all(rows, 'wide', split_axis=0, concat_axis=0, tiled=True)  22 us
    ppermute x10, waiting for transfers between devices, swap(): return lax.ppermute(part, 'wide', [(i, i ^ apart) for i in range(peers)])  21.6 us
    pallas_call x1, Pallas kernels, second_call(): call(second_kernel, [SCALARS] * 2 + [VECTORS] * 5, [(VECTORS, (rows, D),...  15.5 us
    pallas_call x1, Pallas kernels, third_call(): call(third_kernel, [SCALARS] * 2 + [VECTORS] * 6 + [REMAIN] * 3, [(VECTOR...  13.2 us
    ppermute x10, starting transfers between devices, swap(): return lax.ppermute(part, 'wide', [(i, i ^ apart) for i in range(peers)])  9.91 us
    pallas_call x1, Pallas kernels, first_call(): call(first_kernel, [SCALARS] + [VECTORS] * 4, [(VECTORS, (rows, D), bf16)...  8.8 us
    all_to_all x1, starting transfers between devices, exchange(): return lax.all_to_all(rows, 'wide', split_axis=0, concat_axis=0, tiled=True)  4.09 us
  transfers between devices with their start and end apart: 11, of which 9 were waited for; matrix products, arithmetic and copies ran while one was open for 1% of the time, Pallas kernels for 13%

profile of v5, /device:TPU:0, one launch (start us, length us, event | category | flops | bytes accessed | tf_op | source)
XLA Modules:
  0.0 100.2 jit_solution(6654761989596117589)
XLA Ops:
  0.6 8.8 %shard_map.153 = (bf16[2048,128]{1,0:T(8,128)(2,1)}, f32[8,8,256]{2,1,0:T(8,128)}, bf16[8,8,256,256]{3,2,1,0:T(8,128)(2,1)}, bf16[8,384,256]{2,1,0:T(8,128)(2,1)}, bf16[8,256,128]{2,1,0:T(8,128)(2,1)}) custom-call(s32[2048]{0:T(1024)} %order_ref.3, bf16[2048,128]{1,0:T(8,128)(2,1)} %x_ref.3, f32[1,128]{1,0:T(1,128)} %bitcast.13, bf16[128,384]{1,0:T(8,128)(2,1)} %w_ref.5, ...), custom_call_target="tpu_custom_call" | custom-call | tf_op jit(solution)/shard_map/pallas_call | solution.py:357
  9.4 22.0 %all_to_all.23 = bf16[16,128,128]{2,1,0:T(8,128)(2,1)} all-to-all(bf16[16,128,128]{2,1,0:T(8,128)(2,1)} %bitcast.12), channel_id=1, replica_groups=mesh['wide'=16,'grp'=2] {'wide'}, dimensions={0} | all-to-all | bytes 1048576 | tf_op jit(solution)/shard_map/all_to_all | solution.py:425
  31.4 15.5 %shard_map.154 = (bf16[2048,128]{1,0:T(8,128)(2,1)}, f32[272,128]{1,0:T(8,128)}, bf16[272,128]{1,0:T(8,128)(2,1)}) custom-call(s32[1]{0:T(128)} %bitcast.core_ref, s32[2048]{0:T(1024)} %order_ref.2, bf16[2048,128]{1,0:T(8,128)(2,1)} %bitcast.9, bf16[2048,128]{1,0:T(8,128)(2,1)} %d_out_ref.1, f32[1,128]{1,0:T(1,128)} %bitcast.15, bf16[128,384]{1,0:T(8,128)(2,1)} %w_ref.4, ...), custom_call_target="tpu_custom_call" | custom-call | tf_op jit(solution)/shard_map/pallas_call | solution.py:372
  46.9 4.1 %all-to-all-start.1 = ((bf16[16,128,128]{2,1,0:T(8,128)(2,1)}), bf16[16,128,128]{2,1,0:T(8,128)(2,1)S(1)}, u32[]{:S(2)}, u32[]{:S(2)}) async-start(bf16[16,128,128]{2,1,0:T(8,128)(2,1)} %bitcast.11), calls=%async_computation.1 | async-start | bytes 1048576 | tf_op jit(solution)/shard_map/all_to_all | solution.py:425
  51.0 0.4 collective-permute-start
  51.4 1.1 %collective-permute-done = bf16[272,128]{1,0:T(8,128)(2,1)S(1)} collective-permute-done((bf16[272,128]{1,0:T(8,128)(2,1)}, bf16[272,128]{1,0:T(8,128)(2,1)S(1)}, u32[]{:S(2)}, u32[]{:S(2)}) %collective-permute-start) | collective-permute-done | bytes 69664 | tf_op jit(solution)/shard_map/ppermute | solution.py:429
  52.5 0.9 add_convert_fusion.5
  53.4 1.9 %collective-permute-start.1 = (bf16[272,128]{1,0:T(8,128)(2,1)S(1)}, bf16[272,128]{1,0:T(8,128)(2,1)S(1)}, u32[]{:S(2)}, u32[]{:S(2)}) collective-permute-start(bf16[272,128]{1,0:T(8,128)(2,1)S(1)} %add_convert_fusion.5), channel_id=1, source_target_pairs={{0,4},{2,6},{4,0},{6,2},{8,12},{10,14},{12,8},{14,10},{16,20},{18,... | collective-permute-start | bytes 208904 | tf_op jit(solution)/shard_map/ppermute | solution.py:429
  55.4 3.7 %collective-permute-done.1 = bf16[272,128]{1,0:T(8,128)(2,1)S(1)} collective-permute-done((bf16[272,128]{1,0:T(8,128)(2,1)S(1)}, bf16[272,128]{1,0:T(8,128)(2,1)S(1)}, u32[]{:S(2)}, u32[]{:S(2)}) %collective-permute-start.1) | collective-permute-done | bytes 69664 | tf_op jit(solution)/shard_map/ppermute | solution.py:429
  59.1 2.3 %collective-permute-start.2 = (bf16[272,128]{1,0:T(8,128)(2,1)S(1)}, bf16[272,128]{1,0:T(8,128)(2,1)S(1)}, u32[]{:S(2)}, u32[]{:S(2)}) collective-permute-start(bf16[272,128]{1,0:T(8,128)(2,1)S(1)} %add_convert_fusion.4), channel_id=1, source_target_pairs={{0,8},{2,10},{4,12},{6,14},{8,0},{10,2},{12,4},{14,6},{16,24},{18,... | collective-permute-start | bytes 208904 | tf_op jit(solution)/shard_map/ppermute | solution.py:429
  61.4 3.2 %collective-permute-done.2 = bf16[272,128]{1,0:T(8,128)(2,1)S(1)} collective-permute-done((bf16[272,128]{1,0:T(8,128)(2,1)S(1)}, bf16[272,128]{1,0:T(8,128)(2,1)S(1)}, u32[]{:S(2)}, u32[]{:S(2)}) %collective-permute-start.2) | collective-permute-done | bytes 69664 | tf_op jit(solution)/shard_map/ppermute | solution.py:429
  64.7 1.1 %all-to-all-done.1 = bf16[16,128,128]{2,1,0:T(8,128)(2,1)S(1)} async-done(((bf16[16,128,128]{2,1,0:T(8,128)(2,1)}), bf16[16,128,128]{2,1,0:T(8,128)(2,1)S(1)}, u32[]{:S(2)}, u32[]{:S(2)}) %all-to-all-start.1) | async-done | bytes 524320 | tf_op jit(solution)/shard_map/all_to_all | solution.py:425
  65.8 0.0 copy-start
  65.8 1.9 %collective-permute-start.3 = (bf16[272,128]{1,0:T(8,128)(2,1)S(1)}, bf16[272,128]{1,0:T(8,128)(2,1)S(1)}, u32[]{:S(2)}, u32[]{:S(2)}) collective-permute-start(bf16[272,128]{1,0:T(8,128)(2,1)S(1)} %convert_add_fusion.1), channel_id=1, source_target_pairs={{0,16},{2,18},{4,20},{6,22},{8,24},{10,26},{12,28},{14,30},{16,0},... | collective-permute-start | bytes 208904 | tf_op jit(solution)/shard_map/ppermute | solution.py:429
  67.7 0.0 copy-done
  67.7 13.2 %shard_map.155 = (bf16[2048,128]{1,0:T(8,128)(2,1)}, f32[272,128]{1,0:T(8,128)}, bf16[272,128]{1,0:T(8,128)(2,1)}) custom-call(s32[1]{0:T(128)} %bitcast.core_ref, s32[2048]{0:T(1024)} %order_ref.3, bf16[2048,128]{1,0:T(8,128)(2,1)} %bitcast.10, bf16[2048,128]{1,0:T(8,128)(2,1)} %x_ref.3, f32[1,128]{1,0:T(1,128)} %bitcast.14, bf16[128,384]{1,0:T(8,128)(2,1)} %w_ref.5, ...), custom_call_target="tpu_custom_call" | custom-call | tf_op jit(solution)/shard_map/pallas_call | solution.py:397
  80.9 0.0 collective-permute-done.3
  80.9 0.1 collective-permute-start.4
  81.0 1.5 %collective-permute-done.4 = bf16[272,128]{1,0:T(8,128)(2,1)S(1)} collective-permute-done((bf16[272,128]{1,0:T(8,128)(2,1)}, bf16[272,128]{1,0:T(8,128)(2,1)S(1)}, u32[]{:S(2)}, u32[]{:S(2)}) %collective-permute-start.4) | collective-permute-done | bytes 69664 | tf_op jit(solution)/shard_map/ppermute | solution.py:429
  82.5 0.9 add_convert_fusion.3
  83.4 0.4 collective-permute-start.5
  83.8 3.9 %collective-permute-done.5 = bf16[272,128]{1,0:T(8,128)(2,1)S(1)} collective-permute-done((bf16[272,128]{1,0:T(8,128)(2,1)S(1)}, bf16[272,128]{1,0:T(8,128)(2,1)S(1)}, u32[]{:S(2)}, u32[]{:S(2)}) %collective-permute-start.5) | collective-permute-done | bytes 69664 | tf_op jit(solution)/shard_map/ppermute | solution.py:429
  87.8 1.7 %collective-permute-start.6 = (bf16[272,128]{1,0:T(8,128)(2,1)S(1)}, bf16[272,128]{1,0:T(8,128)(2,1)S(1)}, u32[]{:S(2)}, u32[]{:S(2)}) collective-permute-start(bf16[272,128]{1,0:T(8,128)(2,1)S(1)} %add_convert_fusion.2), channel_id=1, source_target_pairs={{0,8},{2,10},{4,12},{6,14},{8,0},{10,2},{12,4},{14,6},{16,24},{18,... | collective-permute-start | bytes 208904 | tf_op jit(solution)/shard_map/ppermute | solution.py:429
  89.5 2.7 %collective-permute-done.6 = bf16[272,128]{1,0:T(8,128)(2,1)S(1)} collective-permute-done((bf16[272,128]{1,0:T(8,128)(2,1)S(1)}, bf16[272,128]{1,0:T(8,128)(2,1)S(1)}, u32[]{:S(2)}, u32[]{:S(2)}) %collective-permute-start.6) | collective-permute-done | bytes 69664 | tf_op jit(solution)/shard_map/ppermute | solution.py:429
  92.2 1.1 %collective-permute-start.7 = (bf16[272,128]{1,0:T(8,128)(2,1)S(1)}, bf16[272,128]{1,0:T(8,128)(2,1)S(1)}, u32[]{:S(2)}, u32[]{:S(2)}) collective-permute-start(bf16[272,128]{1,0:T(8,128)(2,1)S(1)} %add_convert_fusion.1), channel_id=1, source_target_pairs={{0,16},{2,18},{4,20},{6,22},{8,24},{10,26},{12,28},{14,30},{16,0},... | collective-permute-start | bytes 208904 | tf_op jit(solution)/shard_map/ppermute | solution.py:429
  93.3 0.0 collective-permute-start.9
  93.3 4.2 %collective-permute-done.7 = bf16[272,128]{1,0:T(8,128)(2,1)S(1)} collective-permute-done((bf16[272,128]{1,0:T(8,128)(2,1)S(1)}, bf16[272,128]{1,0:T(8,128)(2,1)S(1)}, u32[]{:S(2)}, u32[]{:S(2)}) %collective-permute-start.7) | collective-permute-done | bytes 69664 | tf_op jit(solution)/shard_map/ppermute | solution.py:429
  97.5 0.1 collective-permute-start.8
  97.6 0.0 collective-permute-done.9.came_b
  97.6 1.2 %collective-permute-done.8.came_a = bf16[272,128]{1,0:T(8,128)(2,1)S(1)} collective-permute-done((bf16[272,128]{1,0:T(8,128)(2,1)S(1)}, bf16[272,128]{1,0:T(8,128)(2,1)S(1)}, u32[]{:S(2)}, u32[]{:S(2)}) %collective-permute-start.8) | collective-permute-done | bytes 69664 | tf_op jit(solution)/shard_map/ppermute | solution.py:429
  98.8 1.2 %shard_map.156 = (f32[1,128]{1,0:T(1,128)}, f32[128,384]{1,0:T(8,128)}, f32[128,128]{1,0:T(8,128)}, f32[1,128]{1,0:T(1,128)}, f32[128,384]{1,0:T(8,128)}, /*index=5*/f32[128,128]{1,0:T(8,128)}) custom-call(s32[1]{0:T(128)} %bitcast.core_ref, bf16[272,128]{1,0:T(8,128)(2,1)S(1)} %add_convert_fusion.mine_a, ...), custom_call_target="tpu_custom_call" | custom-call | tf_op jit(solution)/shard_map/pallas_call | solution.py:415
  (6 shorter events, 0.1 us)
Async XLA Ops:
  46.9 18.9 %all-to-all-start.1 = ((bf16[16,128,128]{2,1,0:T(8,128)(2,1)}), bf16[16,128,128]{2,1,0:T(8,128)(2,1)S(1)}, u32[]{:S(2)}, u32[]{:S(2)}) async-start(bf16[16,128,128]{2,1,0:T(8,128)(2,1)} %bitcast.11), calls=%async_computation.1 | async-start | bytes 1048576 | tf_op jit(solution)/shard_map/all_to_all | solution.py:425
  51.0 1.5 %collective-permute-start = (bf16[272,128]{1,0:T(8,128)(2,1)}, bf16[272,128]{1,0:T(8,128)(2,1)S(1)}, u32[]{:S(2)}, u32[]{:S(2)}) collective-permute-start(bf16[272,128]{1,0:T(8,128)(2,1)} %get-tuple-element.36), channel_id=1, source_target_pairs={{0,2},{2,0},{4,6},{6,4},{8,10},{10,8},{12,14},{14,12},{16,18},{18,... | collective-permute-start | bytes 208904 | tf_op jit(solution)/shard_map/ppermute | solution.py:429
  53.4 5.6 %collective-permute-start.1 = (bf16[272,128]{1,0:T(8,128)(2,1)S(1)}, bf16[272,128]{1,0:T(8,128)(2,1)S(1)}, u32[]{:S(2)}, u32[]{:S(2)}) collective-permute-start(bf16[272,128]{1,0:T(8,128)(2,1)S(1)} %add_convert_fusion.5), channel_id=1, source_target_pairs={{0,4},{2,6},{4,0},{6,2},{8,12},{10,14},{12,8},{14,10},{16,20},{18,... | collective-permute-start | bytes 208904 | tf_op jit(solution)/shard_map/ppermute | solution.py:429
  59.1 5.6 %collective-permute-start.2 = (bf16[272,128]{1,0:T(8,128)(2,1)S(1)}, bf16[272,128]{1,0:T(8,128)(2,1)S(1)}, u32[]{:S(2)}, u32[]{:S(2)}) collective-permute-start(bf16[272,128]{1,0:T(8,128)(2,1)S(1)} %add_convert_fusion.4), channel_id=1, source_target_pairs={{0,8},{2,10},{4,12},{6,14},{8,0},{10,2},{12,4},{14,6},{16,24},{18,... | collective-permute-start | bytes 208904 | tf_op jit(solution)/shard_map/ppermute | solution.py:429
  65.8 1.9 %copy-start = (bf16[16,128,128]{2,1,0:T(8,128)(2,1)}, bf16[16,128,128]{2,1,0:T(8,128)(2,1)S(1)}, u32[]{:S(2)}) copy-start(bf16[16,128,128]{2,1,0:T(8,128)(2,1)S(1)} %all-to-all-done.1) | copy-start | bytes 1572868
  65.8 15.1 %collective-permute-start.3 = (bf16[272,128]{1,0:T(8,128)(2,1)S(1)}, bf16[272,128]{1,0:T(8,128)(2,1)S(1)}, u32[]{:S(2)}, u32[]{:S(2)}) collective-permute-start(bf16[272,128]{1,0:T(8,128)(2,1)S(1)} %convert_add_fusion.1), channel_id=1, source_target_pairs={{0,16},{2,18},{4,20},{6,22},{8,24},{10,26},{12,28},{14,30},{16,0},... | collective-permute-start | bytes 208904 | tf_op jit(solution)/shard_map/ppermute | solution.py:429
  80.9 1.5 %collective-permute-start.4 = (bf16[272,128]{1,0:T(8,128)(2,1)}, bf16[272,128]{1,0:T(8,128)(2,1)S(1)}, u32[]{:S(2)}, u32[]{:S(2)}) collective-permute-start(bf16[272,128]{1,0:T(8,128)(2,1)} %get-tuple-element.47), channel_id=1, source_target_pairs={{0,2},{2,0},{4,6},{6,4},{8,10},{10,8},{12,14},{14,12},{16,18},{18,... | collective-permute-start | bytes 208904 | tf_op jit(solution)/shard_map/ppermute | solution.py:429
  83.4 4.4 %collective-permute-start.5 = (bf16[272,128]{1,0:T(8,128)(2,1)S(1)}, bf16[272,128]{1,0:T(8,128)(2,1)S(1)}, u32[]{:S(2)}, u32[]{:S(2)}) collective-permute-start(bf16[272,128]{1,0:T(8,128)(2,1)S(1)} %add_convert_fusion.3), channel_id=1, source_target_pairs={{0,4},{2,6},{4,0},{6,2},{8,12},{10,14},{12,8},{14,10},{16,20},{18,... | collective-permute-start | bytes 208904 | tf_op jit(solution)/shard_map/ppermute | solution.py:429
  87.8 4.4 %collective-permute-start.6 = (bf16[272,128]{1,0:T(8,128)(2,1)S(1)}, bf16[272,128]{1,0:T(8,128)(2,1)S(1)}, u32[]{:S(2)}, u32[]{:S(2)}) collective-permute-start(bf16[272,128]{1,0:T(8,128)(2,1)S(1)} %add_convert_fusion.2), channel_id=1, source_target_pairs={{0,8},{2,10},{4,12},{6,14},{8,0},{10,2},{12,4},{14,6},{16,24},{18,... | collective-permute-start | bytes 208904 | tf_op jit(solution)/shard_map/ppermute | solution.py:429
  92.2 5.3 %collective-permute-start.7 = (bf16[272,128]{1,0:T(8,128)(2,1)S(1)}, bf16[272,128]{1,0:T(8,128)(2,1)S(1)}, u32[]{:S(2)}, u32[]{:S(2)}) collective-permute-start(bf16[272,128]{1,0:T(8,128)(2,1)S(1)} %add_convert_fusion.1), channel_id=1, source_target_pairs={{0,16},{2,18},{4,20},{6,22},{8,24},{10,26},{12,28},{14,30},{16,0},... | collective-permute-start | bytes 208904 | tf_op jit(solution)/shard_map/ppermute | solution.py:429
  93.3 4.3 %collective-permute-start.9 = (bf16[272,128]{1,0:T(8,128)(2,1)S(1)}, bf16[272,128]{1,0:T(8,128)(2,1)S(1)}, u32[]{:S(2)}, u32[]{:S(2)}) collective-permute-start(bf16[272,128]{1,0:T(8,128)(2,1)S(1)} %convert_add_fusion.mine_b), channel_id=1, source_target_pairs={{0,2},{2,0},{4,6},{6,4},{8,10},{10,8},{12,14},{14,12},{16,18},{18,... | collective-permute-start | bytes 208904 | tf_op jit(solution)/shard_map/ppermute | solution.py:429
  97.5 1.3 %collective-permute-start.8 = (bf16[272,128]{1,0:T(8,128)(2,1)S(1)}, bf16[272,128]{1,0:T(8,128)(2,1)S(1)}, u32[]{:S(2)}, u32[]{:S(2)}) collective-permute-start(bf16[272,128]{1,0:T(8,128)(2,1)S(1)} %add_convert_fusion.mine_a), channel_id=1, source_target_pairs={{0,2},{2,0},{4,6},{6,4},{8,10},{10,8},{12,14},{14,12},{16,18},{18,... | collective-permute-start | bytes 208904 | tf_op jit(solution)/shard_map/ppermute | solution.py:429
